TPU v7x, 32 devices: a whole 2x2x4 slice. The times are simulated.
32 devices in a mesh: front: 4 (over z), row: 4 (over y, x), col: 2 (over core).
Axes of the slice: x: 2, y: 2, z: 4, core: 2. Of those that a mesh axis runs over, the one named last changes fastest.
Arguments:
- front_matrix: float32 [4, 24, 512, 3072], P('front', None, 'row', 'col')
- front_sizes: int32 [4], P('front'), may hold values from 8192 to 12288, as said below
- contrib: float32 [4, 4, 512, 3072], P('front', None, 'row', 'col'), may hold values from -6 to 6
- dest_front: int32 [4, 4, 4], P('front', None, 'row'), may hold values from 0 to 3, as said below
- dest_local: int32 [4, 4, 4], P('front', None, 'row'), may hold values from 2 to 23, as said below
Outputs:
- factored: float32 [4, 24, 512, 3072], P('front', None, 'row', 'col')
Inputs may be any that keep to these rules, and one draw needn't show every extreme that they name: `front_sizes`: multiples of 128; every draw has a front of order 12288 and one of order 8192. For each (g, r), the 4 entries dest_front[g, :, r] name distinct fronts. The block (g, k, r) lands on parent rows from (dest_local * 4 + r) * 128: at or after row 1024 and wholly below the parent's order; several blocks may land on the same rows; in every draw some block lands in the last round of blocks of the largest front.
All inputs are finite; a program needn't handle non-finite values.
Results may differ from a plain program's by a relative error of at most 0.0003.
Values sent between devices are 32-bit elements; how exact they have to be, the bound alone decides.
No kernel may reach another device: no remote copies, remote signals or barrier semaphores. Data moves between devices by JAX's collectives and lax.ppermute only.
A program may use at most 128 MiB of HBM per device.

v0:
```python
import jax
import jax.numpy as jnp
from jax import lax
from jax.sharding import PartitionSpec as P

PW = 512
NPANEL = 2
W = 3072


def broadcast(value, axis, source):
    kept = jnp.where(lax.axis_index(axis) == source, value, 0).astype(value.dtype)
    return lax.psum(kept, axis)


def lower_inverse(pivot_block):
    symmetric = jnp.tril(pivot_block) + jnp.tril(pivot_block, -1).T
    factor = jnp.linalg.cholesky(symmetric)
    eye_block = jnp.eye(factor.shape[0], dtype=jnp.float32)
    inverse = jax.scipy.linalg.solve_triangular(factor, eye_block, lower=True)
    return (factor, inverse)


def on_device(front_matrix, front_sizes, contrib, dest_front, dest_local):
    front_count = lax.axis_size("front")
    row_count = lax.axis_size("row")
    row_here = lax.axis_index("row")
    col_here = lax.axis_index("col")
    local_blocks = front_matrix.shape[1]
    block_rows = front_matrix.shape[2]
    half_width = front_matrix.shape[3]
    half_rows = block_rows // 2
    cycle_rows = row_count * block_rows
    local_rows = local_blocks * block_rows
    window_blocks = W // cycle_rows
    block_ids = jnp.arange(local_blocks, dtype=jnp.int32)
    global_row = (
        block_ids[:, None] * cycle_rows
        + row_here * block_rows
        + jnp.arange(block_rows, dtype=jnp.int32)[None, :]
    ).reshape(local_rows)
    global_col = col_here * half_width + jnp.arange(half_width, dtype=jnp.int32)
    matrix = front_matrix[0].reshape(local_rows, half_width)
    matrix = jnp.where((global_row < front_sizes[0])[:, None], matrix, 0.0)
    targets = dest_front[0, :, 0]
    places = dest_local[0, :, 0]
    fronts_all = jnp.arange(front_count, dtype=jnp.int32)
    select = targets[None, :] == fronts_all[:, None]
    outgoing = jnp.einsum(
        "fk,kiw->fiw", select.astype(jnp.float32), contrib[0], precision=lax.Precision.HIGHEST
    )
    slot_place = jnp.where(
        jnp.any(select, axis=1), jnp.sum(jnp.where(select, places[None, :], 0), axis=1), -1
    )
    incoming, in_place = (
        lax.all_to_all(outgoing, "front", split_axis=0, concat_axis=0, tiled=True),
        lax.all_to_all(slot_place, "front", split_axis=0, concat_axis=0, tiled=True),
    )
    placing = (in_place[None, :] == block_ids[:, None]).astype(jnp.float32)
    placed_rows = jnp.einsum("ls,siw->liw", placing, incoming, precision=lax.Precision.HIGHEST)
    matrix = matrix + placed_rows.reshape(local_rows, half_width)
    for panel_index in range(NPANEL):
        col_start = panel_index * PW
        owned_columns = matrix[:, col_start : col_start + PW]
        columns = broadcast(owned_columns, "col", 0)
        first_block = col_start // block_rows
        pivot_block = first_block // row_count
        offset = first_block % row_count * block_rows
        col_blocks = columns.reshape(local_blocks, block_rows, PW)
        row_piece = lax.dynamic_slice_in_dim(
            col_blocks[pivot_block], col_here * half_rows, half_rows, 0
        )
        gathered = lax.all_gather(row_piece, ("row", "col"), axis=0, tiled=True)
        factor, inverse = lower_inverse(gathered[offset : offset + PW])
        solved = jnp.dot(columns, inverse.T, precision=lax.Precision.HIGHEST)
        solved = jnp.where((global_row < col_start)[:, None], 0.0, solved)
        global_first = (pivot_block * row_count + row_here) * block_rows
        in_pivot = (global_first >= col_start) & (global_first < col_start + PW)
        pivot_piece = lax.dynamic_slice_in_dim(
            factor, jnp.clip(global_first - col_start, 0, PW - block_rows), block_rows, 0
        )
        current = solved[pivot_block * block_rows : (pivot_block + 1) * block_rows]
        solved = solved.at[pivot_block * block_rows : (pivot_block + 1) * block_rows].set(
            jnp.where(in_pivot, pivot_piece, current)
        )
        solved_blocks = solved.reshape(local_blocks, block_rows, PW)
        row_piece = lax.dynamic_slice_in_dim(
            solved_blocks[:window_blocks], col_here * half_rows, half_rows, 1
        )
        window_factor = lax.all_gather(row_piece, ("row", "col"), axis=1, tiled=True).reshape(W, PW)
        mine_cols = lax.dynamic_slice_in_dim(window_factor, col_here * half_width, half_width, 0)
        update = jnp.dot(solved, mine_cols.T, precision=lax.Precision.HIGHEST)
        active = (global_row >= col_start + PW)[:, None] & (global_col >= col_start + PW)[None, :]
        matrix = matrix - jnp.where(active, update, 0.0)
        replaced = jnp.where(col_here == 0, solved, matrix[:, col_start : col_start + PW])
        matrix = matrix.at[:, col_start : col_start + PW].set(replaced)
    upper_part = (global_row < NPANEL * PW)[:, None] & (global_col >= NPANEL * PW)[None, :]
    matrix = jnp.where(upper_part, 0.0, matrix)
    return matrix.reshape(1, local_blocks, block_rows, half_width)


def solution(mesh):
    return jax.shard_map(
        on_device,
        mesh=mesh,
        in_specs=(
            P("front", None, "row", "col"),
            P("front"),
            P("front", None, "row", "col"),
            P("front", None, "row"),
            P("front", None, "row"),
        ),
        out_specs=P("front", None, "row", "col"),
        check_vma=False,
    )
```

profile of v0, /device:TPU:1, one launch (start us, length us, event | category | flops | bytes accessed | tf_op | source)
XLA Modules:
  0.0 804.7 jit_solution(1992277852820637262)
XLA Ops:
  27.7 68.7 %all-to-all-done.1 = f32[4,128,1536]{2,1,0:T(8,128)S(1)} async-done(((f32[4,128,1536]{2,1,0:T(8,128)}), f32[4,128,1536]{2,1,0:T(8,128)S(1)}, u32[]{:S(2)}, u32[]{:S(2)}) %all-to-all-start.1) | async-done | bytes 3145760 | tf_op jit(solution)/shard_map/all_to_all | solution.py:56
  105.4 21.3 %copy.26 = f32[24,128,1536]{2,1,0:T(8,128)} copy(f32[24,128,1536]{2,0,1:T(8,128)S(1)} %fusion.2) | data formatting | bytes 37748736 | tf_op jit(solution)/shard_map/ls,siw->liw/dot_general | solution.py:60
  126.7 12.7 %bitcast_add_fusion = f32[3072,1536]{1,0:T(8,128)S(1)} fusion(f32[24,128,1536]{2,1,0:T(8,128)} %copy.26, f32[1,24,128,1536]{3,2,1,0:T(8,128)} %param.16, pred[3072]{0:T(1024)(128)(4,1)S(1)} %get-tuple-element.120), kind=kLoop, calls=%fused_computation.4 | loop fusion | flops 9437184 | bytes 56626176 | tf_op jit(solution)/shard_map/add | solution.py:61
  149.8 32.4 %all-reduce.4.cloned.1.call-done = f32[3072,512]{1,0:T(8,128)} async-done(((f32[3072,512]{1,0:T(8,128)}), f32[3072,512]{1,0:T(8,128)}) %all-reduce.4.cloned.1.call-update) | async-done | bytes 6291472 | tf_op jit(solution)/shard_map/psum | solution.py:13
  184.2 24.7 %all-gather.5.cloned.1.call-done = f32[512,512]{1,0:T(8,128)} async-done(((f32[64,512]{1,0:T(8,128)}), f32[512,512]{1,0:T(8,128)}) %all-gather.5.cloned.1.call-update) | async-done | bytes 1048592 | tf_op jit(solution)/shard_map/all_gather | solution.py:73
  213.6 11.7 %cholesky.286 = f32[128,128]{1,0:T(8,128)S(1)} custom-call(f32[128,128]{1,0:T(8,128)S(1)} %cholesky.426), custom_call_target="Cholesky" | custom-call | tf_op jit(solution)/shard_map/jit(cholesky)/cholesky | solution.py:18
  237.8 11.7 %cholesky.305 = f32[128,128]{1,0:T(8,128)S(1)} custom-call(f32[128,128]{1,0:T(8,128)S(1)} %cholesky.430), custom_call_target="Cholesky" | custom-call | tf_op jit(solution)/shard_map/jit(cholesky)/cholesky | solution.py:18
  261.3 11.7 %cholesky.326 = f32[128,128]{1,0:T(8,128)S(1)} custom-call(f32[128,128]{1,0:T(8,128)S(1)} %cholesky.435), custom_call_target="Cholesky" | custom-call | tf_op jit(solution)/shard_map/jit(cholesky)/cholesky | solution.py:18
  285.0 11.9 %cholesky.343 = f32[128,128]{1,0:T(8,128)S(1)} custom-call(f32[128,128]{1,0:T(8,128)S(1)} %convolution_subtract_fusion.11), custom_call_target="Cholesky" | custom-call | tf_op jit(solution)/shard_map/jit(cholesky)/cholesky | solution.py:18
  310.3 39.3 %custom-call.30 = f32[4,128,128]{1,2,0:T(8,128)S(1)} custom-call(f32[4,128,128]{2,1,0:T(8,128)S(1)} %get-tuple-element.69), custom_call_target="InvertDiagBlocksLowerTriangular" | custom-call | tf_op jit(solution)/shard_map/jit(_solve_triangular)/triangular_solve | solution.py:20
  352.8 13.3 %convolution_select_fusion.1 = f32[3072,512]{1,0:T(8,128)S(1)} fusion(f32[3072,512]{1,0:T(8,128)} %all-reduce.4.cloned.1.call-done, pred[3072]{0:T(1024)(128)(4,1)S(1)} %get-tuple-element.118, f32[128,512]{1,0:T(8,128)S(1)} %fusion.72, f32[128,512]{1,0:T(8,128)S(1)} %fusion.73, f32[128,512]{1,0:T(8,128)S(1)} %fusion.75, f32[128,512]{1,0:T(8,128)S(1)} %fusion.50), kind=kOutput, calls=%fused_computation.16 | convolution fusion | flops 9666035712 | bytes 13634560 | tf_op jit(solution)/shard_map/dot_general | solution.py:75
  371.9 44.8 %all-gather.7.cloned.1.call-done = f32[6,512,512]{2,1,0:T(8,128)} async-done(((f32[6,64,512]{2,1,0:T(8,128)}), f32[6,512,512]{2,1,0:T(8,128)}) %all-gather.7.cloned.1.call-update) | async-done | bytes 6291472 | tf_op jit(solution)/shard_map/all_gather | solution.py:90
  416.7 37.2 %select_subtract_fusion.1 = f32[3072,1536]{1,0:T(8,128)} fusion(f32[3072,1536]{1,0:T(8,128)} %copy-done.2, f32[3072,512]{1,0:T(8,128)} %copy-done.3, pred[1536]{0:T(1024)(128)(4,1)S(1)} %fusion.96, pred[3072]{0:T(1024)(128)(4,1)S(1)} %get-tuple-element.119, f32[3072,512]{1,0:T(8,128)} %bitcast.143, s32[]{:T(128)S(6)} %select_n.117), kind=kOutput, calls=%fused_computation.7 | convolution fusion | flops 29005185024 | bytes 47190532 | tf_op jit(solution)/shard_map/dot_general | solution.py:92
  467.8 33.9 %all-reduce.6.cloned.1.call-done = f32[3072,512]{1,0:T(8,128)} async-done(((f32[3072,512]{1,0:T(8,128)}), f32[3072,512]{1,0:T(8,128)}) %all-reduce.6.cloned.1.call-update) | async-done | bytes 6291472 | tf_op jit(solution)/shard_map/psum | solution.py:13
  504.4 23.9 %all-gather.9.cloned.1.call-done = f32[512,512]{1,0:T(8,128)} async-done(((f32[64,512]{1,0:T(8,128)}), f32[512,512]{1,0:T(8,128)}) %all-gather.9.cloned.1.call-update) | async-done | bytes 1048592 | tf_op jit(solution)/shard_map/all_gather | solution.py:73
  533.0 11.7 %cholesky.358 = f32[128,128]{1,0:T(8,128)S(1)} custom-call(f32[128,128]{1,0:T(8,128)S(1)} %cholesky.439), custom_call_target="Cholesky" | custom-call | tf_op jit(solution)/shard_map/jit(cholesky)/cholesky | solution.py:18
  557.2 11.7 %cholesky.377 = f32[128,128]{1,0:T(8,128)S(1)} custom-call(f32[128,128]{1,0:T(8,128)S(1)} %cholesky.443), custom_call_target="Cholesky" | custom-call | tf_op jit(solution)/shard_map/jit(cholesky)/cholesky | solution.py:18
  581.8 11.7 %cholesky.398 = f32[128,128]{1,0:T(8,128)S(1)} custom-call(f32[128,128]{1,0:T(8,128)S(1)} %cholesky.448), custom_call_target="Cholesky" | custom-call | tf_op jit(solution)/shard_map/jit(cholesky)/cholesky | solution.py:18
  605.5 11.9 %cholesky.415 = f32[128,128]{1,0:T(8,128)S(1)} custom-call(f32[128,128]{1,0:T(8,128)S(1)} %convolution_subtract_fusion.10), custom_call_target="Cholesky" | custom-call | tf_op jit(solution)/shard_map/jit(cholesky)/cholesky | solution.py:18
  630.0 39.3 %custom-call.34 = f32[4,128,128]{1,2,0:T(8,128)S(1)} custom-call(f32[4,128,128]{2,1,0:T(8,128)S(1)} %get-tuple-element.70), custom_call_target="InvertDiagBlocksLowerTriangular" | custom-call | tf_op jit(solution)/shard_map/jit(_solve_triangular)/triangular_solve | solution.py:20
  672.5 13.4 %convolution_select_fusion = f32[3072,512]{1,0:T(8,128)S(1)} fusion(f32[3072,512]{1,0:T(8,128)} %all-reduce.6.cloned.1.call-done, pred[3072]{0:T(1024)(128)(4,1)S(1)} %get-tuple-element.116, f32[128,512]{1,0:T(8,128)S(1)} %fusion.66, f32[128,512]{1,0:T(8,128)S(1)} %fusion.67, f32[128,512]{1,0:T(8,128)S(1)} %fusion.69, f32[128,512]{1,0:T(8,128)S(1)} %fusion.48), kind=kOutput, calls=%fused_computation.15 | convolution fusion | flops 9666035712 | bytes 13634560 | tf_op jit(solution)/shard_map/dot_general | solution.py:75
  691.4 45.0 %all-gather.11.cloned.1.call-done = f32[6,512,512]{2,1,0:T(8,128)} async-done(((f32[6,64,512]{2,1,0:T(8,128)}), f32[6,512,512]{2,1,0:T(8,128)}) %all-gather.11.cloned.1.call-update) | async-done | bytes 6291472 | tf_op jit(solution)/shard_map/all_gather | solution.py:90
  736.4 37.5 %select_subtract_fusion = f32[3072,1536]{1,0:T(8,128)} fusion(f32[3072,1536]{1,0:T(8,128)} %fusion, f32[3072,512]{1,0:T(8,128)} %copy-done.4, pred[1536]{0:T(1024)(128)(4,1)S(1)} %fusion.97, pred[3072]{0:T(1024)(128)(4,1)S(1)} %get-tuple-element.117, f32[3072,512]{1,0:T(8,128)} %bitcast.144, s32[]{:T(128)S(6)} %select_n.117), kind=kOutput, calls=%fused_computation.6 | convolution fusion | flops 29005185024 | bytes 47190532 | tf_op jit(solution)/shard_map/dot_general | solution.py:92
  781.7 15.8 %and_select_fusion = f32[3072,1536]{1,0:T(8,128)} fusion(f32[3072,1536]{1,0:T(8,128)} %fusion.1, pred[1536]{0:T(1024)(128)(4,1)S(1)} %fusion.97, pred[3072]{0:T(1024)(128)(4,1)S(1)} %get-tuple-element.115), kind=kLoop, calls=%fused_computation.8 | loop fusion | flops 9437184 | bytes 37753344 | tf_op jit(solution)/shard_map/jit(_where)/select_n | solution.py:98
  (157 shorter events, 203.5 us)
Async XLA Ops:
  6.5 7.9 copy-start
  9.0 12.7 %all-to-all-start = ((s32[4,1,1]{2,1,0:T(1,128)}), s32[4,1,1]{2,1,0:T(1,128)S(1)}, u32[]{:S(2)}, u32[]{:S(2)}) async-start(s32[4,1,1]{2,1,0:T(1,128)} %copy.22), calls=%async_computation | async-start | bytes 4096 | tf_op jit(solution)/shard_map/all_to_all | solution.py:57
  21.7 74.7 %all-to-all-start.1 = ((f32[4,128,1536]{2,1,0:T(8,128)}), f32[4,128,1536]{2,1,0:T(8,128)S(1)}, u32[]{:S(2)}, u32[]{:S(2)}) async-start(f32[4,128,1536]{2,1,0:T(8,128)} %copy.24), calls=%async_computation.1 | async-start | bytes 6291456 | tf_op jit(solution)/shard_map/all_to_all | solution.py:56
  26.2 155.9 %all-reduce.4.cloned.1.call-start = ((), (), s32[]{:S(2)}) async-start(), calls=%async_computation.2 | async-start | bytes 12582912 | tf_op jit(solution)/shard_map/psum | solution.py:13
  139.4 6.9 copy-start.2
  149.7 59.3 %all-gather.5.cloned.1.call-start = ((), (), s32[]{:S(2)}) async-start(), calls=%async_computation.3 | async-start | bytes 1179648 | tf_op jit(solution)/shard_map/all_gather | solution.py:73
  183.8 232.8 %all-gather.7.cloned.1.call-start = ((), (), s32[]{:S(2)}) async-start(), calls=%async_computation.4 | async-start | bytes 7077888 | tf_op jit(solution)/shard_map/all_gather | solution.py:90
  212.5 1.0 copy-start.6
  367.2 2.7 copy-start.3
  371.0 130.7 %all-reduce.6.cloned.1.call-start = ((), (), s32[]{:S(2)}) async-start(), calls=%async_computation.5 | async-start | bytes 12582912 | tf_op jit(solution)/shard_map/psum | solution.py:13
  467.8 60.5 %all-gather.9.cloned.1.call-start = ((), (), s32[]{:S(2)}) async-start(), calls=%async_computation.6 | async-start | bytes 1179648 | tf_op jit(solution)/shard_map/all_gather | solution.py:73
  503.4 233.0 %all-gather.11.cloned.1.call-start = ((), (), s32[]{:S(2)}) async-start(), calls=%async_computation.7 | async-start | bytes 7077888 | tf_op jit(solution)/shard_map/all_gather | solution.py:90
  532.0 1.0 copy-start.5
  686.9 2.7 copy-start.4
  781.6 15.8 %copy-start.1 = (f32[1,4,128,1536]{3,2,1,0:T(8,128)S(1)}, f32[1,4,128,1536]{3,2,1,0:T(8,128)}, u32[]{:S(2)}) copy-start(f32[1,4,128,1536]{3,2,1,0:T(8,128)} %param.18) | copy-start | bytes 9437188
Sparse Core Ops, SparseCore 0:
  149.8 32.3 all-reduce.3
  184.2 24.7 all-gather.4
  371.1 45.4 all-gather.6
  467.9 33.8 all-reduce.5
  503.5 24.7 all-gather.8
  690.9 45.4 all-gather.10
where the time goes:
time: 811 us; the launch traced here: 805 us
  other arithmetic  303 us (37%)
  waiting for transfers between devices  274 us (34%)
  matrix products  132 us (16%)
  local copies, waits for them, and re-layouts  63.8 us (8%)
  between operations  20.2 us (2%)
  starting transfers between devices  11.5 us (1%)
    another operation x29, other arithmetic, lower_inverse(): factor = jnp.linalg.cholesky(symmetric)  158 us
    all_gather x2, waiting for transfers between devices, on_device(): lax.all_gather(row_piece, ('row', 'col'), axis=1, tiled=True).reshape(W, PW)  89.7 us
    another operation x5, other arithmetic, lower_inverse(): inverse = jax.scipy.linalg.solve_triangular(factor, eye_block, lower=True)  81.2 us
    dot_general x2, matrix products, on_device(): update = jnp.dot(solved, mine_cols.T, precision=lax.Precision.HIGHEST)  74.8 us
    all_to_all x1, waiting for transfers between devices, on_device(): lax.all_to_all(outgoing, 'front', split_axis=0, concat_axis=0, tiled=True)  68.7 us
    psum x2, waiting for transfers between devices, broadcast(): return lax.psum(kept, axis)  66.3 us
    all_gather x2, waiting for transfers between devices, on_device(): gathered = lax.all_gather(row_piece, ('row', 'col'), axis=0, tiled=True)  48.7 us
    dot_general x2, matrix products, on_device(): solved = jnp.dot(columns, inverse.T, precision=lax.Precision.HIGHEST)  26.7 us
  transfers between devices with their start and end apart: 8, of which 7 were waited for; matrix products, arithmetic and copies ran while one was open for 1% of the time, Pallas kernels for 0%

commit v1 on v0

v1 whole, which is shorter than its diff:
```python
import functools

import jax
import jax.numpy as jnp
from jax import lax
from jax.experimental import pallas as pl
from jax.experimental.pallas import tpu as pltpu
from jax.sharding import PartitionSpec as P

PW = 512
NPANEL = 2
B = 128
KP = PW * NPANEL
NB = PW // B
EXT = B + 8
NT = ((1,), (1,))
NN = ((1,), (0,))
TN = ((0,), (0,))
F32 = jnp.float32
BF16 = jnp.bfloat16
VMEM_LIMIT = 56 * 2**20


def split(x):
    high = x.astype(BF16)
    return high, (x - high.astype(F32)).astype(BF16)


def dot3(a, b, dims):
    def one(u, v):
        return lax.dot_general(u, v, (dims, ((), ())), preferred_element_type=F32)

    return one(a[0], b[0]) + (one(a[0], b[1]) + one(a[1], b[0]))


def dot6(a, b, dims):
    return lax.dot_general(
        a, b, (dims, ((), ())), precision=lax.Precision.HIGHEST, preferred_element_type=F32
    )


def over_lanes(group, lane):
    return jnp.broadcast_to(group[:, lane : lane + 1], group.shape)


def over_rows(group, row):
    return jnp.broadcast_to(group[row : row + 1, :], group.shape)


def factor_block(s_ref, v_ref, u_ref):
    sub = lax.broadcasted_iota(jnp.int32, (8, B), 0)
    lane = lax.broadcasted_iota(jnp.int32, (8, B), 1)
    n = B // 8
    left = [s_ref[8 * g : 8 * g + 8, :] for g in range(n)]
    right = [jnp.where(lane == sub + 8 * g, 1.0, 0.0).astype(F32) for g in range(n)]
    for b in range(n):
        cols = [[over_lanes(left[g], 8 * b + j) for j in range(8)] for g in range(b, n)]
        scale = jnp.ones((8, B), F32)
        for j in range(8):
            pivot = over_rows(cols[0][j], j)
            inv = 1.0 / pivot
            lrow = over_rows(left[b], j)
            rrow = over_rows(right[b], j)
            krow = [over_rows(cols[0][k], j) if k > j else None for k in range(8)]
            scale = jnp.where(sub == j, lax.rsqrt(pivot), scale)
            for g in range(b, n):
                f = cols[g - b][j] * inv
                if g == b:
                    f = jnp.where(sub > j, f, 0.0)
                for k in range(j + 1, 8):
                    cols[g - b][k] = cols[g - b][k] - f * krow[k]
                left[g] = left[g] - f * lrow
                right[g] = right[g] - f * rrow
        u_ref[8 * b : 8 * b + 8, :] = jnp.where(lane >= sub + 8 * b, left[b] * scale, 0.0)
        v_ref[8 * b : 8 * b + 8, :] = right[b] * scale


def panel_factor(m_ref, u_ref, v_ref):
    def body(k, _):
        c = pl.multiple_of(k * B, B)
        factor_block(m_ref.at[pl.ds(c, B), pl.ds(c, B)], v_ref, u_ref)
        row = dot6(v_ref[...], m_ref[pl.ds(c, B), :], NN)
        m_ref[pl.ds(c, B), :] = row
        m_ref[pl.ds(c, B), pl.ds(c, B)] = u_ref[...]
        for i in range(1, NB):

            @pl.when(i > k)
            def _():
                up = m_ref[pl.ds(c, B), i * B : (i + 1) * B]
                rows = slice(i * B, (i + 1) * B)
                m_ref[rows, :] = m_ref[rows, :] - dot6(up, row, TN)

        return 0

    lax.fori_loop(0, NB, body, 0)


def load_symmetric(a_ref, m_ref, col):
    r = lax.broadcasted_iota(jnp.int32, (B, B), 0)
    c = lax.broadcasted_iota(jnp.int32, (B, B), 1)
    for i in range(NB):
        for j in range(NB):
            here = (slice(i * B, (i + 1) * B), slice(PW + j * B, PW + (j + 1) * B))
            m_ref[here] = jnp.where(r == c, 1.0, 0.0) if i == j else jnp.zeros((B, B), F32)
            if j > i:
                continue
            block = a_ref[i * B : (i + 1) * B, col + j * B : col + (j + 1) * B]
            if i == j:
                block = jnp.where(r >= c, block, block.T)
                m_ref[i * B : (i + 1) * B, i * B : (i + 1) * B] = block
            else:
                m_ref[i * B : (i + 1) * B, j * B : (j + 1) * B] = block
                m_ref[j * B : (j + 1) * B, i * B : (i + 1) * B] = block.T


def store_factor(m_ref, l_ref, i_ref):
    for i in range(NB):
        for j in range(NB):
            here = (slice(i * B, (i + 1) * B), slice(j * B, (j + 1) * B))
            if j <= i:
                l_ref[here] = m_ref[j * B : (j + 1) * B, i * B : (i + 1) * B].T
            else:
                l_ref[here] = jnp.zeros((B, B), F32)
    i_ref[...] = m_ref[:, PW:]


class Copies:
    def __init__(self, sems):
        self.sems, self.count = sems, 0

    def start(self, src, dst, when=None):
        copy = pltpu.make_async_copy(src, dst, self.sems.at[self.count])
        self.count += 1
        if when is None:
            copy.start()
        else:
            pl.when(when)(copy.start)
        return copy, when

    @staticmethod
    def wait(started):
        for copy, when in started:
            if when is None:
                copy.wait()
            else:
                pl.when(when)(copy.wait)


def take_rows(copies, me, pieces, dst, first, count, pick, cols):
    started = []
    rows = len(pieces)
    for k, piece in enumerate(pieces):
        for l, src in pick(piece):
            at = (me ^ k) + l * rows - first
            low, high = l * rows - first, l * rows - first + rows - 1
            inside = None if low >= 0 and high < count else (at >= 0) & (at < count)
            clipped = at if inside is None else jnp.clip(at, 0, count - 1)
            here = pl.ds(pl.multiple_of(clipped * B, B), B)
            started.append(copies.start(src, dst.at[here, cols], inside))
    return started


class Sizes:
    def __init__(self, rows, fronts, per_device, blocks_here, half):
        self.rows, self.fronts, self.kb = rows, fronts, per_device
        self.blocks, self.half = blocks_here, half
        self.npl = KP // (rows * B)
        self.g = max(1, blocks_here // 6)
        self.tiles = blocks_here // self.g
        self.windows = 2 * half // (rows * B) - self.npl
        self.pivot_first = 0 if self.npl == 2 else NB
        self.n0 = rows + 1 if rows == 4 and self.windows % 2 == 0 else rows
        self.a_first = KP // B
        self.a_count = (half - KP) // B
        self.b_first = half // B
        self.b_count = half // B

    def narrow_at(self, d):
        width = self.half - KP
        per = KP // width
        return (pl.ds(self.half - KP + d // per * B, B), pl.ds(d % per * width, width))

    def window_blocks(self, first, count):
        return range(first // self.rows - self.npl, (first + count - 1) // self.rows + 1 - self.npl)


def gathered(z, refs):
    if len(refs) == z.rows:
        return [lambda l, ref=ref: ref.at[l] for ref in refs]
    half = z.windows // 2
    whole, (first, second) = refs[: z.rows - 1], refs[z.rows - 1 :]
    across = lambda l: first.at[l] if l < half else second.at[l - half]
    return [lambda l, ref=ref: ref.at[l] for ref in whole] + [across]


def route(z, info, dest, d):
    front = lax.rem(info[3] + d, z.fronts)
    slot, place = jnp.int32(0), jnp.int32(-1)
    for k in range(z.kb):
        hit = dest[k] == front
        slot = jnp.where(hit, k, slot)
        place = jnp.where(hit, dest[z.kb + k], place)
    return slot, place


def read_places(z, blocks, places):
    for d in range(z.fronts):
        places[d] = jnp.max(blocks[d, B:EXT, :B]).astype(jnp.int32)


def factor0_kernel(z, info, *refs):
    pieces, (l_out, i_out, a_ref, m_ref, u_ref, v_ref, sems) = refs[: z.rows], refs[z.rows :]

    @pl.when(info[0] == 0)
    def _():
        copies = Copies(sems)
        pick = lambda piece: [(0, piece.at[:, pl.ds(0, PW)])]
        copies.wait(take_rows(copies, info[1], pieces, a_ref, 0, NB, pick, slice(None)))
        load_symmetric(a_ref, m_ref, 0)
        panel_factor(m_ref, u_ref, v_ref)
        store_factor(m_ref, l_out, i_out)


def middle_kernel(z, info, i0_ref, *refs):
    pieces, (out, a_ref, f_s, sems) = refs[: z.rows], refs[z.rows :]

    @pl.when(info[0] == 0)
    def _():
        copies = Copies(sems)
        pick = lambda piece: [(0, piece.at[:, pl.ds(0, PW)])]
        started = take_rows(copies, info[1], pieces, a_ref, z.pivot_first, NB, pick, slice(None))
        started.append(copies.start(i0_ref, f_s.at[:, pl.ds(0, PW)]))
        copies.wait(started)
        f_s[:, PW:] = dot6(a_ref[...], f_s[:, :PW], NT)
        copies.wait(
            [copies.start(f_s.at[pl.ds(n * B, B)], out.at[n, pl.ds(0, B)]) for n in range(NB)]
        )


def take_factor(copies, packed, f_s):
    return [copies.start(packed.at[n, pl.ds(0, B)], f_s.at[pl.ds(n * B, B)]) for n in range(NB)]


def sort_kernel(z, info, dest, first, second, *refs):
    f = z.fronts
    panel, late = refs[:f], refs[f : 2 * f]
    c_s, e_s, sems = refs[2 * f :]
    narrow = z.half - KP

    @pl.when(info[0] == 1)
    def _():
        copies = Copies(sems)
        routes = [route(z, info, dest, d) for d in range(f)]
        order = list(range(1, f)) + [0]
        reads = {}
        for d in order:
            slot, place = routes[d]
            c_s[d, B:EXT, :B] = jnp.full((EXT - B, B), place.astype(F32))
            reads[d] = copies.start(first.at[slot, :, pl.ds(0, KP)], c_s.at[d, pl.ds(0, B)])
        more = []
        for d in order:
            slot = routes[d][0]
            more.append(
                copies.start(first.at[slot, :, pl.ds(KP, narrow)], e_s.at[d, :, pl.ds(0, narrow)])
            )
            more.append(copies.start(second.at[slot], e_s.at[d, :, pl.ds(narrow, z.half)]))
        writes = []
        for d in order:
            copies.wait([reads[d]])
            writes.append(copies.start(c_s.at[d], panel[d]))
        for n, d in enumerate(order):
            copies.wait(more[2 * n : 2 * n + 2])
            writes.append(copies.start(e_s.at[d], late[d]))
        copies.wait(writes)


def window_kernel(z, info, other, _, *refs):
    f = z.fronts
    panel, (h0, h1, back), (t_ref, c_ref, places, sems) = refs[:f], refs[f : f + 3], refs[f + 3 :]

    @pl.when(info[0] == 1)
    def _():
        copies = Copies(sems)
        started = [copies.start(other.at[pl.ds(z.npl, z.windows), :, pl.ds(0, KP)], t_ref)]
        started += [copies.start(panel[d], c_ref.at[d]) for d in range(f)]
        copies.wait(started)
        later = [copies.start(c_ref, back)]
        read_places(z, c_ref, places)
        for d in range(f):
            place = places[d] - z.npl

            @pl.when((place >= 0) & (place < z.windows))
            def _():
                t_ref[place] += c_ref[d, :B]

        later.append(copies.start(t_ref.at[:, :, pl.ds(0, PW)], h0))
        later.append(copies.start(t_ref.at[:, :, pl.ds(PW, PW)], h1))
        copies.wait(later)


def fill_panel(z, info, places, blocks, i, p_ref, t_ref):
    for l in range(z.g):
        lb = i * z.g + l
        valid = (lb * z.rows + info[1]) * B < info[2]
        t_ref[l * B : (l + 1) * B, :] = jnp.where(valid, p_ref[l, :, :KP], 0.0)
    for d in range(z.fronts):
        at = places[d] - i * z.g

        @pl.when((at >= 0) & (at < z.g))
        def _():
            here = pl.ds(pl.multiple_of(at * B, B), B)
            t_ref[here, :] += blocks[d, :B]


def both_kernel(z, info, mine, theirs, *refs):
    pivots, w0, refs = refs[: z.rows], refs[z.rows : z.rows + z.n0], refs[z.rows + z.n0 :]
    p_ref, x_ref, l_out, i_out, t_out, p_high, p_low, z_out = refs[:8]
    a_ref, f_s, i_s, m_ref, u_ref, v_ref, w_s, t_s, c_s, inv, y, places, sems = refs[8:]
    i = pl.program_id(0)

    @pl.when((info[0] == 0) & (i == 0))
    def _():
        copies = Copies(sems)
        pick = lambda piece: [(0, piece.at[:, pl.ds(PW, PW)])]
        started = take_rows(copies, info[1], pivots, a_ref, z.pivot_first, NB, pick, slice(None))
        started += take_factor(copies, mine, f_s)
        copies.wait(started)
        load_symmetric(a_ref, m_ref, 0)
        m_ref[:, :PW] = m_ref[:, :PW] - dot6(f_s[:, PW:], f_s[:, PW:], NT)
        panel_factor(m_ref, u_ref, v_ref)
        store_factor(m_ref, l_out, i_s)
        copies.wait([copies.start(i_s, i_out.at[pl.ds(0, PW), pl.ds(0, PW)])])

    @pl.when(info[0] == 1)
    def _():
        @pl.when(i == 0)
        def _():
            copies = Copies(sems)
            used = z.window_blocks(z.b_first, z.b_count)
            pick = lambda piece: [(l + z.npl, piece(l)) for l in used]
            started = take_rows(copies, info[1], gathered(z, w0), w_s, z.b_first, z.b_count, pick, slice(None))
            started += take_factor(copies, theirs, f_s)
            started.append(copies.start(mine, c_s))
            copies.wait(started)
            read_places(z, c_s, places)
            inv[0], inv[1] = split(f_s[:, :PW])
            inverse = (inv[0], inv[1])
            z_out[0], z_out[1] = split(dot3(split(f_s[:, PW:]), inverse, NN))
            for n in range(z.half // PW):
                span = slice(n * PW, (n + 1) * PW)
                x = split(dot3(split(w_s[span, :]), inverse, NT))
                y[0, span, :], y[1, span, :] = split(dot3(x, inverse, NN))

        fill_panel(z, info, places, c_s, i, p_ref, t_s)
        p = split(t_s[:, :PW])
        high, low = split(t_s[:, PW:] - dot3(p, (z_out[0], z_out[1]), NT))
        p_high[...] = high.reshape(p_high.shape)
        p_low[...] = low.reshape(p_low.shape)
        for n in range(z.half // PW):
            span = slice(n * PW, (n + 1) * PW)
            update = dot3(p, (y[0, span, :], y[1, span, :]), NT)
            for l in range(z.g):
                valid = ((i * z.g + l) * z.rows + info[1]) * B < info[2]
                t_out[l, :, span] = (
                    jnp.where(valid, x_ref[l, :, span], 0.0) - update[l * B : (l + 1) * B]
                )


def pick_kernel(z, info, *refs):
    w0, w1, refs = refs[: z.n0], refs[z.n0 : z.n0 + z.rows], refs[z.n0 + z.rows :]
    late, (_, out, w_s, sems) = refs[: z.fronts], refs[z.fronts :]
    narrow = z.half - KP

    @pl.when(info[0] == 1)
    def _():
        copies = Copies(sems)
        used = z.window_blocks(z.a_first, z.a_count)
        pick = lambda piece: [(l + z.npl, piece(l)) for l in used]
        started = []
        for n, pieces in enumerate((w0, w1)):
            cols = pl.ds(n * PW, PW)
            started += take_rows(
                copies, info[1], gathered(z, pieces), w_s, z.a_first, z.a_count, pick, cols
            )
        for d in range(z.fronts):
            started.append(copies.start(late[d].at[:, pl.ds(0, narrow)], w_s.at[z.narrow_at(d)]))
        copies.wait(started)
        copies.wait([copies.start(w_s, out)])


def final_kernel(z, info, mine, theirs, mine2, theirs2, l0_ref, l1_ref, z_ref, *refs):
    f = z.fronts
    w0, w1, refs = refs[: z.n0], refs[z.n0 : z.n0 + z.rows], refs[z.n0 + z.rows :]
    late, refs = refs[:f], refs[f:]
    x_ref, t_ref, p_high, p_low, out = refs[:5]
    t_s, c_s, w_s, e_s, i_s, s_s, inv, y, places, sems = refs[5:]
    i = pl.program_id(0)

    def add_late(cols):
        for d in range(f):
            at = places[d] - i * z.g

            @pl.when((at >= 0) & (at < z.g))
            def _():
                out[at, :, cols] += e_s[d, :, cols]

    @pl.when(info[0] == 0)
    def _():
        copies = Copies(sems)
        right = pl.ds(KP, z.half - KP)

        @pl.when(i == 0)
        def _():
            started = [
                copies.start(theirs2.at[pl.ds(0, PW), :], w_s.at[pl.ds(0, PW), :]),
                copies.start(mine2.at[pl.ds(0, PW), pl.ds(0, PW)], i_s),
                copies.start(theirs, c_s),
            ]
            started += take_factor(copies, mine, s_s)
            started += [copies.start(theirs2.at[z.narrow_at(d)], e_s.at[d, :, right]) for d in range(f)]
            copies.wait(started)
            read_places(z, c_s, places)
            for n, value in enumerate((s_s[:, :PW], s_s[:, PW:], i_s[...])):
                inv[n, 0], inv[n, 1] = split(value)
            x = split(dot3(split(w_s[:PW, :PW]), (inv[0, 0], inv[0, 1]), NT))
            inv[3, 0], inv[3, 1] = x
            later = split(w_s[:PW, PW:] - dot3(x, (inv[1, 0], inv[1, 1]), NT))
            inv[4, 0], inv[4, 1] = split(dot3(later, (inv[2, 0], inv[2, 1]), NT))

        fill_panel(z, info, places, c_s, i, x_ref, t_s)
        x0 = dot3(split(t_s[:, :PW]), (inv[0, 0], inv[0, 1]), NT)
        x0s = split(x0)
        later = split(t_s[:, PW:] - dot3(x0s, (inv[1, 0], inv[1, 1]), NT))
        x1 = dot3(later, (inv[2, 0], inv[2, 1]), NT)
        update = dot3(x0s, (inv[3, 0], inv[3, 1]), NT) + dot3(split(x1), (inv[4, 0], inv[4, 1]), NT)
        for l in range(z.g):
            span = slice(l * B, (l + 1) * B)
            valid = ((i * z.g + l) * z.rows + info[1]) * B < info[2]
            out[l, :, :PW] = x0[span]
            out[l, :, PW:KP] = x1[span]
            out[l, :, KP:] = jnp.where(valid, x_ref[l, :, KP:], 0.0) - update[span]
        add_late(slice(KP, z.half))

        @pl.when(i == 0)
        def _():
            for l in range(z.npl):
                row = (l * z.rows + info[1]) * B
                out[l, :, PW:] = jnp.zeros((B, z.half - PW), F32)

                @pl.when(row < PW)
                def _():
                    here = pl.ds(pl.multiple_of(row, B), B)
                    copy = pltpu.make_async_copy(l0_ref.at[here], out.at[l, :, pl.ds(0, PW)], sems.at[0])
                    copy.start()
                    copy.wait()

                @pl.when(row >= PW)
                def _():
                    here = pl.ds(pl.multiple_of(row - PW, B), B)
                    piece = (row - PW) // B
                    first = pltpu.make_async_copy(mine.at[piece, pl.ds(0, B), pl.ds(PW, PW)], out.at[l, :, pl.ds(0, PW)], sems.at[0])
                    second = pltpu.make_async_copy(l1_ref.at[here], out.at[l, :, pl.ds(PW, PW)], sems.at[1])
                    first.start()
                    second.start()
                    first.wait()
                    second.wait()

    @pl.when(info[0] == 1)
    def _():
        copies = Copies(sems)

        @pl.when(i == 0)
        def _():
            used = z.window_blocks(z.b_first, z.b_count)
            pick = lambda piece: [(l + z.npl, piece(l)) for l in used]
            started = [copies.start(theirs2.at[pl.ds(0, PW), pl.ds(0, PW)], i_s)]
            started.append(copies.start(z_ref, inv.at[1]))
            started.append(copies.start(mine.at[:, pl.ds(B, EXT - B)], c_s.at[:, pl.ds(B, EXT - B)]))
            for n, pieces in enumerate((w0, w1)):
                cols = pl.ds(n * PW, PW)
                started += take_rows(
                    copies, info[1], gathered(z, pieces), w_s, z.b_first, z.b_count, pick, cols
                )
            right = pl.ds(z.half - KP, z.half)
            arriving = [copies.start(late[d].at[:, right], e_s.at[d]) for d in range(f)]
            copies.wait(started)
            read_places(z, c_s, places)
            inv[0, 0], inv[0, 1] = split(i_s[...])
            inverse = (inv[0, 0], inv[0, 1])
            for n in range(z.half // PW):
                span = slice(n * PW, (n + 1) * PW)
                w = w_s[span, PW:] - dot3(split(w_s[span, :PW]), (inv[1, 0], inv[1, 1]), NT)
                x = split(dot3(split(w), inverse, NT))
                y[0, span, :], y[1, span, :] = split(dot3(x, inverse, NN))
            copies.wait(arriving)

        p = (p_high[...].reshape(z.g * B, PW), p_low[...].reshape(z.g * B, PW))
        for n in range(z.half // PW):
            span = slice(n * PW, (n + 1) * PW)
            update = dot3(p, (y[0, span, :], y[1, span, :]), NT)
            for l in range(z.g):
                out[l, :, span] = t_ref[l, :, span] - update[l * B : (l + 1) * B]
        add_late(slice(0, z.half))

        @pl.when(i == 0)
        def _():
            for l in range(z.npl):
                out[l] = jnp.zeros((B, z.half), F32)


ANY = pl.BlockSpec(memory_space=pl.ANY)
WHOLE = pl.BlockSpec(memory_space=pltpu.VMEM)
SCALARS = pl.BlockSpec(memory_space=pltpu.SMEM)
PARAMS = pltpu.CompilerParams(vmem_limit_bytes=VMEM_LIMIT)


def shape(*dims, dtype=F32):
    return jax.ShapeDtypeStruct(dims, dtype)


def after(value, *others):
    return lax.optimization_barrier((value, *others))[0]


def on_device(front_matrix, front_sizes, contrib, dest_front, dest_local):
    fronts = lax.axis_size("front")
    rows = lax.axis_size("row")
    front_here = lax.axis_index("front")
    row_here = lax.axis_index("row")
    col_here = lax.axis_index("col")
    matrix = front_matrix[0]
    blocks = contrib[0]
    blocks_here, _, half = matrix.shape
    z = Sizes(rows, fronts, blocks.shape[0], blocks_here, half)

    def from_rows(x, core):
        return [x] + [along_rows(x, k, core) for k in range(1, rows)]

    def along_rows(x, k, core):
        pairs = [(r * 2 + core, (r ^ k) * 2 + core) for r in range(rows)]
        return lax.ppermute(x, ("row", "col"), pairs)

    def along_fronts(x, d, source, target):
        pairs = [(f * 2 + source, (f + d) % fronts * 2 + target) for f in range(fronts)]
        return lax.ppermute(x, ("front", "col"), pairs)

    def to_other(x):
        return lax.ppermute(x, "col", [(0, 1)])

    def swap(x):
        return lax.ppermute(x, "col", [(0, 1), (1, 0)])

    info = jnp.concatenate(
        [
            jnp.stack([col_here, row_here]).astype(jnp.int32),
            front_sizes,
            front_here.astype(jnp.int32)[None],
        ]
    )
    dest = jnp.concatenate([dest_front[0, :, 0], dest_local[0, :, 0]])

    q0 = matrix[0, :, :PW]
    if z.npl == 2:
        pivot0 = from_rows(q0, 0)
    other_blocks = to_other(blocks)
    other = to_other(after(matrix, other_blocks))
    pivot1 = from_rows(matrix[z.npl - 1, :, :KP], 0)
    if z.npl != 2:
        pivot0 = pivot1

    factor_scratch = [
        pltpu.VMEM((PW, PW), F32),
        pltpu.VMEM((PW, 2 * PW), F32),
        pltpu.VMEM((B, B), F32),
        pltpu.VMEM((B, B), F32),
    ]
    l0, i0 = pl.pallas_call(
        functools.partial(factor0_kernel, z),
        out_shape=[shape(PW, PW)] * 2,
        in_specs=[SCALARS] + [ANY] * rows,
        out_specs=[WHOLE] * 2,
        scratch_shapes=factor_scratch + [pltpu.SemaphoreType.DMA((rows,))],
        compiler_params=PARAMS,
        name="factor0",
    )(info, *pivot0)
    packed = pl.pallas_call(
        functools.partial(middle_kernel, z),
        out_shape=shape(fronts, EXT, KP),
        in_specs=[SCALARS] + [ANY] * (rows + 1),
        out_specs=ANY,
        scratch_shapes=[
            pltpu.VMEM((PW, PW), F32),
            pltpu.VMEM((PW, 2 * PW), F32),
            pltpu.SemaphoreType.DMA((rows + NB + 1,)),
        ],
        compiler_params=PARAMS,
        name="middle",
    )(info, i0, *pivot1)

    refs = pl.pallas_call(
        functools.partial(sort_kernel, z),
        out_shape=[shape(EXT, KP)] * fronts + [shape(B, 2 * half - KP)] * fronts,
        in_specs=[SCALARS] * 2 + [ANY] * 2,
        out_specs=[ANY] * (2 * fronts),
        scratch_shapes=[
            pltpu.VMEM((fronts, EXT, KP), F32),
            pltpu.VMEM((fronts, B, 2 * half - KP), F32),
            pltpu.SemaphoreType.DMA((5 * fronts,)),
        ],
        compiler_params=PARAMS,
        name="sort",
    )(info, dest, after(other_blocks, packed), blocks)
    panel, late = list(refs[:fronts]), list(refs[fronts:])
    panel = panel[:1] + [along_fronts(x, d + 1, 1, 1) for d, x in enumerate(panel[1:])]
    h0, h1, mine = pl.pallas_call(
        functools.partial(window_kernel, z),
        out_shape=[shape(z.windows, B, PW)] * 2 + [shape(fronts, EXT, KP)],
        in_specs=[SCALARS] + [ANY] * (fronts + 2),
        out_specs=[ANY] * 3,
        input_output_aliases={2: 2},
        scratch_shapes=[
            pltpu.VMEM((z.windows, B, KP), F32),
            pltpu.VMEM((fronts, EXT, KP), F32),
            pltpu.SMEM((fronts,), jnp.int32),
            pltpu.SemaphoreType.DMA((fronts + 4,)),
        ],
        compiler_params=PARAMS,
        name="window",
    )(info, other, packed, *panel)
    if z.n0 == rows:
        w0 = from_rows(h0, 1)
    else:
        middle = z.windows // 2
        sides = [along_rows(h0, 1, 1), along_rows(h0, 2, 1)]
        across = [along_rows(sides[0][:middle], 2, 1), along_rows(sides[1][middle:], 1, 1)]
        w0 = [h0, *sides, *across]
    late = late[:1] + [along_fronts(after(x, h0), d + 1, 1, 1) for d, x in enumerate(late[1:])]
    theirs = swap(after(mine, *w0))
    w1 = from_rows(after(h1, *w0), 1)

    def tile(width, core):
        return pl.BlockSpec((z.g, B, width), lambda i, s: (jnp.where(s[0] == core, i, 0), 0, 0))

    both = pltpu.VMEM((2, PW, PW), BF16)
    rest = half - KP + -(-fronts * (half - KP) // KP) * B
    l1, mine2, trailing, p_high, p_low, z_pair = pl.pallas_call(
        functools.partial(both_kernel, z),
        out_shape=[
            shape(PW, PW),
            shape(rest, KP),
            shape(blocks_here, B, half),
            shape(blocks_here, B, PW, dtype=BF16),
            shape(blocks_here, B, PW, dtype=BF16),
            shape(2, PW, PW, dtype=BF16),
        ],
        grid_spec=pltpu.PrefetchScalarGridSpec(
            num_scalar_prefetch=1,
            grid=(z.tiles,),
            in_specs=[ANY] * (2 + rows + z.n0) + [tile(KP, 1), tile(half, 1)],
            out_specs=[WHOLE, ANY, tile(half, 1), tile(PW, 1), tile(PW, 1), WHOLE],
            scratch_shapes=factor_scratch[:1]
            + [pltpu.VMEM((PW, 2 * PW), F32), pltpu.VMEM((PW, PW), F32)]
            + factor_scratch[1:]
            + [
                pltpu.VMEM((half, PW), F32),
                pltpu.VMEM((z.g * B, KP), F32),
                pltpu.VMEM((fronts, EXT, KP), F32),
                both,
                pltpu.VMEM((2, half, PW), BF16),
                pltpu.SMEM((fronts,), jnp.int32),
                pltpu.SemaphoreType.DMA((rows * z.windows + NB + 2,)),
            ],
        ),
        compiler_params=PARAMS,
        name="factor1_update0",
    )(info, mine, theirs, *pivot1, *w0, other, matrix)

    mine2 = pl.pallas_call(
        functools.partial(pick_kernel, z),
        out_shape=shape(rest, KP),
        in_specs=[SCALARS] + [ANY] * (z.n0 + rows + fronts + 1),
        out_specs=ANY,
        scratch_shapes=[
            pltpu.VMEM((rest, KP), F32),
            pltpu.SemaphoreType.DMA((2 * rows * z.windows + fronts + 1,)),
        ],
        input_output_aliases={1 + z.n0 + rows + fronts: 0},
        compiler_params=PARAMS,
        name="pick",
    )(info, *w0, *w1, *late, mine2)
    theirs2 = swap(mine2)

    out = pl.pallas_call(
        functools.partial(final_kernel, z),
        out_shape=shape(blocks_here, B, half),
        grid_spec=pltpu.PrefetchScalarGridSpec(
            num_scalar_prefetch=1,
            grid=(z.tiles,),
            in_specs=[ANY] * (7 + z.n0 + rows + fronts)
            + [tile(half, 0), tile(half, 1), tile(PW, 1), tile(PW, 1)],
            out_specs=pl.BlockSpec((z.g, B, half), lambda i, s: (i, 0, 0)),
            scratch_shapes=[
                pltpu.VMEM((z.g * B, KP), F32),
                pltpu.VMEM((fronts, EXT, KP), F32),
                pltpu.VMEM((half, KP), F32),
                pltpu.VMEM((fronts, B, half), F32),
                pltpu.VMEM((PW, PW), F32),
                pltpu.VMEM((PW, 2 * PW), F32),
                pltpu.VMEM((5, 2, PW, PW), BF16),
                pltpu.VMEM((2, half, PW), BF16),
                pltpu.SMEM((fronts,), jnp.int32),
                pltpu.SemaphoreType.DMA((2 * rows * z.windows + fronts + 8,)),
            ],
        ),
        compiler_params=PARAMS,
        name="final",
    )(info, mine, theirs, mine2, theirs2, l0, l1, z_pair, *w0, *w1, *late, matrix, trailing, p_high, p_low)
    return out[None]


def solution(mesh):
    return jax.shard_map(
        on_device,
        mesh=mesh,
        in_specs=(
            P("front", None, "row", "col"),
            P("front"),
            P("front", None, "row", "col"),
            P("front", None, "row"),
            P("front", None, "row"),
        ),
        out_specs=P("front", None, "row", "col"),
        check_vma=False,
    )
```

time: 811 us -> 224 us (0.28)
  the two profiles are of different devices: /device:TPU:1 before, /device:TPU:0 now
where the time goes in v1:
time: 224 us; the launch traced here: 220 us
  Pallas kernels  119 us (53%)
  starting transfers between devices  73.7 us (33%)
  waiting for transfers between devices  16.1 us (7%)
  local copies, waits for them, and re-layouts  7.68 us (3%)
    pallas_call x1, Pallas kernels, on_device(): pl.pallas_call(functools.partial(both_kernel, z), out_shape=[shape(PW, PW...  43.1 us
    pallas_call x1, Pallas kernels, on_device(): pl.pallas_call(functools.partial(final_kernel, z), out_shape=shape(blocks...  41.5 us
    ppermute x2, starting transfers between devices, swap(): return lax.ppermute(x, 'col', [(0, 1), (1, 0)])  29.1 us
    ppermute x13, starting transfers between devices, along_rows(): return lax.ppermute(x, ('row', 'col'), pairs)  26.6 us
    pallas_call x1, Pallas kernels, on_device(): pl.pallas_call(functools.partial(factor0_kernel, z), out_shape=[shape(PW,...  26.2 us
    ppermute x2, starting transfers between devices, to_other(): return lax.ppermute(x, 'col', [(0, 1)])  12.8 us
    ppermute x13, waiting for transfers between devices, along_rows(): return lax.ppermute(x, ('row', 'col'), pairs)  6.63 us
    unnamed x38, local copies, waits for them, and re-layouts  5.57 us
  transfers between devices with their start and end apart: 23, of which 3 were waited for; matrix products, arithmetic and copies ran while one was open for 2% of the time, Pallas kernels for 34%

profile of v1, /device:TPU:0, one launch (start us, length us, event | category | flops | bytes accessed | tf_op | source)
XLA Modules:
  0.0 219.7 jit_solution(3047791913553100994)
XLA Ops:
  0.0 4.0 %collective-permute-start = (f32[4,128,1536]{2,1,0:T(8,128)}, f32[4,128,1536]{2,1,0:T(8,128)}, u32[]{:S(2)}, u32[]{:S(2)}) collective-permute-start(f32[4,128,1536]{2,1,0:T(8,128)} %bitcast.17), channel_id=1, source_target_pairs={{0,1},{2,3},{4,5},{6,7},{8,9},{10,11},{12,13},{14,15},{16,17},{18,... | collective-permute-start | bytes 9437192 | tf_op jit(solution)/shard_map/ppermute | solution.py:548
  4.1 3.9 %collective-permute-done.first = f32[4,128,1536]{2,1,0:T(8,128)} collective-permute-done((f32[4,128,1536]{2,1,0:T(8,128)}, f32[4,128,1536]{2,1,0:T(8,128)}, u32[]{:S(2)}, u32[]{:S(2)}) %collective-permute-start) | collective-permute-done | bytes 3145760 | tf_op jit(solution)/shard_map/ppermute | solution.py:548
  8.0 8.7 %collective-permute-start.1 = (f32[24,128,1536]{2,1,0:T(8,128)}, f32[24,128,1536]{2,1,0:T(8,128)}, u32[]{:S(2)}, u32[]{:S(2)}) collective-permute-start(f32[24,128,1536]{2,1,0:T(8,128)} %bitcast.12), channel_id=1, source_target_pairs={{0,1},{2,3},{4,5},{6,7},{8,9},{10,11},{12,13},{14,15},{16,17},{18,... | collective-permute-start | bytes 56623112 | tf_op jit(solution)/shard_map/ppermute | solution.py:548
  17.7 5.2 %collective-permute-start.4 = (f32[128,512]{1,0:T(8,128)S(1)}, f32[128,512]{1,0:T(8,128)S(1)}, u32[]{:S(2)}, u32[]{:S(2)}) collective-permute-start(f32[128,512]{1,0:T(8,128)S(1)} %slice_bitcast_fusion.1.refs_0_), channel_id=1, source_target_pairs={{0,6},{2,4},{4,2},{6,0},{8,14},{10,12},{12,10},{14,8},{16,22},{18,... | collective-permute-start | bytes 786440 | tf_op jit(solution)/shard_map/ppermute | solution.py:541
  22.9 2.4 %collective-permute-start.3 = (f32[128,512]{1,0:T(8,128)S(1)}, f32[128,512]{1,0:T(8,128)S(1)}, u32[]{:S(2)}, u32[]{:S(2)}) collective-permute-start(f32[128,512]{1,0:T(8,128)S(1)} %slice_bitcast_fusion.1.refs_0_), channel_id=1, source_target_pairs={{0,4},{2,6},{4,0},{6,2},{8,12},{10,14},{12,8},{14,10},{16,20},{18,... | collective-permute-start | bytes 786440 | tf_op jit(solution)/shard_map/ppermute | solution.py:541
  25.3 1.1 slice_bitcast_fusion.refs_0_
  26.4 3.4 %collective-permute-start.7 = (f32[128,1024]{1,0:T(8,128)S(1)}, f32[128,1024]{1,0:T(8,128)S(1)}, u32[]{:S(2)}, u32[]{:S(2)}) collective-permute-start(f32[128,1024]{1,0:T(8,128)S(1)} %slice_bitcast_fusion.refs_0_), channel_id=1, source_target_pairs={{0,6},{2,4},{4,2},{6,0},{8,14},{10,12},{12,10},{14,8},{16,22},{18,... | collective-permute-start | bytes 1572872 | tf_op jit(solution)/shard_map/ppermute | solution.py:541
  29.8 1.9 collective-permute-start.6
  31.8 3.9 %collective-permute-start.5 = (f32[128,1024]{1,0:T(8,128)S(1)}, f32[128,1024]{1,0:T(8,128)S(1)}, u32[]{:S(2)}, u32[]{:S(2)}) collective-permute-start(f32[128,1024]{1,0:T(8,128)S(1)} %slice_bitcast_fusion.refs_0_), channel_id=1, source_target_pairs={{0,2},{2,0},{4,6},{6,4},{8,10},{10,8},{12,14},{14,12},{16,18},{18,... | collective-permute-start | bytes 1572872 | tf_op jit(solution)/shard_map/ppermute | solution.py:541
  35.7 2.0 collective-permute-start.2
  38.3 1.3 pad_add_fusion.1.dest
  40.3 6.6 %collective-permute-done.2.refs_1_ = f32[128,512]{1,0:T(8,128)S(1)} collective-permute-done((f32[128,512]{1,0:T(8,128)S(1)}, f32[128,512]{1,0:T(8,128)S(1)}, u32[]{:S(2)}, u32[]{:S(2)}) %collective-permute-start.2) | collective-permute-done | bytes 262176 | tf_op jit(solution)/shard_map/ppermute | solution.py:541
  47.6 26.2 %factor0.1 = (f32[512,512]{1,0:T(8,128)}, f32[512,512]{1,0:T(8,128)}) custom-call(s32[4]{0:T(128)} %pad_add_fusion.info, f32[128,512]{1,0:T(8,128)} %copy-done.12, f32[128,512]{1,0:T(8,128)} %copy-done.18, f32[128,512]{1,0:T(8,128)} %copy-done.17, f32[128,512]{1,0:T(8,128)} %copy-done.16), custom_call_target="tpu_custom_call" | custom-call | tf_op jit(solution)/shard_map/factor0/pallas_call | solution.py:577
  75.0 5.4 %middle.1._ = f32[4,136,1024]{2,1,0:T(8,128)} custom-call(s32[4]{0:T(128)} %pad_add_fusion.info, f32[512,512]{1,0:T(8,128)} %get-tuple-element.32.i0_ref, f32[128,1024]{1,0:T(8,128)} %copy-done.5, f32[128,1024]{1,0:T(8,128)} %copy-done.11, f32[128,1024]{1,0:T(8,128)} %copy-done.10, f32[128,1024]{1,0:T(8,128)} %copy-done.9), custom_call_target="tpu_custom_call" | custom-call | tf_op jit(solution)/shard_map/middle/pallas_call | solution.py:586
  88.4 1.1 collective-permute-start.15
  91.0 1.7 collective-permute-start.21
  92.6 1.6 collective-permute-start.18
  94.3 1.6 collective-permute-start.17
  95.9 1.7 collective-permute-start.16
  97.6 43.1 %factor1_update0.1 = (f32[512,512]{1,0:T(8,128)}, f32[768,1024]{1,0:T(8,128)}, f32[24,128,1536]{2,1,0:T(8,128)}, bf16[24,128,512]{2,1,0:T(8,128)(2,1)}, bf16[24,...) custom-call(s32[4]{0:T(128)} %pad_add_fusion.info, f32[4,136,1024]{2,1,0:T(8,128)} %get-tuple-element.40.mine, ...), custom_call_target="tpu_custom_call" | custom-call | tf_op jit(solution)/shard_map/factor1_update0/pallas_call | solution.py:646
  142.8 28.0 %collective-permute-start.22 = (f32[768,1024]{1,0:T(8,128)}, f32[768,1024]{1,0:T(8,128)S(1)}, u32[]{:S(2)}, u32[]{:S(2)}) collective-permute-start(f32[768,1024]{1,0:T(8,128)} %pick.1.mine2), channel_id=1, source_target_pairs={{0,1},{1,0},{2,3},{3,2},{4,5},{5,4},{6,7},{7,6},{8,9},{9,8},{10,11... | collective-permute-start | bytes 9437192 | tf_op jit(solution)/shard_map/ppermute | solution.py:551
  170.8 5.5 %collective-permute-done.22.theirs2 = f32[768,1024]{1,0:T(8,128)S(1)} collective-permute-done((f32[768,1024]{1,0:T(8,128)}, f32[768,1024]{1,0:T(8,128)S(1)}, u32[]{:S(2)}, u32[]{:S(2)}) %collective-permute-start.22) | collective-permute-done | bytes 3145760 | tf_op jit(solution)/shard_map/ppermute | solution.py:551
  176.3 1.6 copy-done.8
  177.9 41.5 %final.1 = f32[24,128,1536]{2,1,0:T(8,128)} custom-call(s32[4]{0:T(128)} %pad_add_fusion.info, f32[4,136,1024]{2,1,0:T(8,128)} %get-tuple-element.40.mine, f32[4,136,1024]{2,1,0:T(8,128)} %copy-done.2, f32[768,1024]{1,0:T(8,128)} %pick.1.mine2, f32[768,1024]{1,0:T(8,128)} %copy-done.8, f32[512,512]{1,0:T(8,128)} %get-tuple-element.51.l0_ref, ...), custom_call_target="tpu_custom_call" | custom-call | tf_op jit(solution)/shard_map/final/pallas_call | solution.py:693
  (73 shorter events, 14.7 us)
Async XLA Ops:
  0.0 8.0 %collective-permute-start = (f32[4,128,1536]{2,1,0:T(8,128)}, f32[4,128,1536]{2,1,0:T(8,128)}, u32[]{:S(2)}, u32[]{:S(2)}) collective-permute-start(f32[4,128,1536]{2,1,0:T(8,128)} %bitcast.17), channel_id=1, source_target_pairs={{0,1},{2,3},{4,5},{6,7},{8,9},{10,11},{12,13},{14,15},{16,17},{18,... | collective-permute-start | bytes 9437192 | tf_op jit(solution)/shard_map/ppermute | solution.py:548
  8.0 75.5 %collective-permute-start.1 = (f32[24,128,1536]{2,1,0:T(8,128)}, f32[24,128,1536]{2,1,0:T(8,128)}, u32[]{:S(2)}, u32[]{:S(2)}) collective-permute-start(f32[24,128,1536]{2,1,0:T(8,128)} %bitcast.12), channel_id=1, source_target_pairs={{0,1},{2,3},{4,5},{6,7},{8,9},{10,11},{12,13},{14,15},{16,17},{18,... | collective-permute-start | bytes 56623112 | tf_op jit(solution)/shard_map/ppermute | solution.py:548
  17.7 14.1 %collective-permute-start.4 = (f32[128,512]{1,0:T(8,128)S(1)}, f32[128,512]{1,0:T(8,128)S(1)}, u32[]{:S(2)}, u32[]{:S(2)}) collective-permute-start(f32[128,512]{1,0:T(8,128)S(1)} %slice_bitcast_fusion.1.refs_0_), channel_id=1, source_target_pairs={{0,6},{2,4},{4,2},{6,0},{8,14},{10,12},{12,10},{14,8},{16,22},{18,... | collective-permute-start | bytes 786440 | tf_op jit(solution)/shard_map/ppermute | solution.py:541
  22.9 12.8 %collective-permute-start.3 = (f32[128,512]{1,0:T(8,128)S(1)}, f32[128,512]{1,0:T(8,128)S(1)}, u32[]{:S(2)}, u32[]{:S(2)}) collective-permute-start(f32[128,512]{1,0:T(8,128)S(1)} %slice_bitcast_fusion.1.refs_0_), channel_id=1, source_target_pairs={{0,4},{2,6},{4,0},{6,2},{8,12},{10,14},{12,8},{14,10},{16,20},{18,... | collective-permute-start | bytes 786440 | tf_op jit(solution)/shard_map/ppermute | solution.py:541
  26.4 47.5 %copy-start.5 = (f32[128,1024]{1,0:T(8,128)}, f32[128,1024]{1,0:T(8,128)S(1)}, u32[]{:S(2)}) copy-start(f32[128,1024]{1,0:T(8,128)S(1)} %slice_bitcast_fusion.refs_0_) | copy-start | bytes 1572868
  26.4 47.4 %collective-permute-start.7 = (f32[128,1024]{1,0:T(8,128)S(1)}, f32[128,1024]{1,0:T(8,128)S(1)}, u32[]{:S(2)}, u32[]{:S(2)}) collective-permute-start(f32[128,1024]{1,0:T(8,128)S(1)} %slice_bitcast_fusion.refs_0_), channel_id=1, source_target_pairs={{0,6},{2,4},{4,2},{6,0},{8,14},{10,12},{12,10},{14,8},{16,22},{18,... | collective-permute-start | bytes 1572872 | tf_op jit(solution)/shard_map/ppermute | solution.py:541
  29.8 44.0 %collective-permute-start.6 = (f32[128,1024]{1,0:T(8,128)S(1)}, f32[128,1024]{1,0:T(8,128)S(1)}, u32[]{:S(2)}, u32[]{:S(2)}) collective-permute-start(f32[128,1024]{1,0:T(8,128)S(1)} %slice_bitcast_fusion.refs_0_), channel_id=1, source_target_pairs={{0,4},{2,6},{4,0},{6,2},{8,12},{10,14},{12,8},{14,10},{16,20},{18,... | collective-permute-start | bytes 1572872 | tf_op jit(solution)/shard_map/ppermute | solution.py:541
  31.8 42.1 %collective-permute-start.5 = (f32[128,1024]{1,0:T(8,128)S(1)}, f32[128,1024]{1,0:T(8,128)S(1)}, u32[]{:S(2)}, u32[]{:S(2)}) collective-permute-start(f32[128,1024]{1,0:T(8,128)S(1)} %slice_bitcast_fusion.refs_0_), channel_id=1, source_target_pairs={{0,2},{2,0},{4,6},{6,4},{8,10},{10,8},{12,14},{14,12},{16,18},{18,... | collective-permute-start | bytes 1572872 | tf_op jit(solution)/shard_map/ppermute | solution.py:541
  35.7 11.2 %collective-permute-start.2 = (f32[128,512]{1,0:T(8,128)S(1)}, f32[128,512]{1,0:T(8,128)S(1)}, u32[]{:S(2)}, u32[]{:S(2)}) collective-permute-start(f32[128,512]{1,0:T(8,128)S(1)} %slice_bitcast_fusion.1.refs_0_), channel_id=1, source_target_pairs={{0,2},{2,0},{4,6},{6,4},{8,10},{10,8},{12,14},{14,12},{16,18},{18,... | collective-permute-start | bytes 786440 | tf_op jit(solution)/shard_map/ppermute | solution.py:541
  81.3 2.1 collective-permute-start.8
  82.0 1.4 collective-permute-start.9
  82.7 0.7 collective-permute-start.10
  85.4 1.5 collective-permute-start.12
  86.1 1.5 collective-permute-start.11
  86.9 1.5 collective-permute-start.14
  87.7 0.7 collective-permute-start.13
  88.4 7.5 %collective-permute-start.15 = (f32[4,136,1024]{2,1,0:T(8,128)}, f32[4,136,1024]{2,1,0:T(8,128)S(1)}, u32[]{:S(2)}, u32[]{:S(2)}) collective-permute-start(f32[4,136,1024]{2,1,0:T(8,128)} %get-tuple-element.40.mine), channel_id=1, source_target_pairs={{0,1},{1,0},{2,3},{3,2},{4,5},{5,4},{6,7},{7,6},{8,9},{9,8},{10,11... | collective-permute-start | bytes 6684680 | tf_op jit(solution)/shard_map/ppermute | solution.py:551
  89.5 4.8 %collective-permute-start.19 = (f32[128,2048]{1,0:T(8,128)}, f32[128,2048]{1,0:T(8,128)S(1)}, u32[]{:S(2)}, u32[]{:S(2)}) collective-permute-start(f32[128,2048]{1,0:T(8,128)} %get-tuple-element.45), channel_id=1, source_target_pairs={{1,9},{9,17},{17,25},{25,1},{3,11},{11,19},{19,27},{27,3},{5,13},{... | collective-permute-start | bytes 3145736 | tf_op jit(solution)/shard_map/ppermute | solution.py:545
  90.2 50.5 %collective-permute-start.20 = (f32[128,2048]{1,0:T(8,128)}, f32[128,2048]{1,0:T(8,128)S(1)}, u32[]{:S(2)}, u32[]{:S(2)}) collective-permute-start(f32[128,2048]{1,0:T(8,128)} %get-tuple-element.47), channel_id=1, source_target_pairs={{1,17},{9,25},{17,1},{25,9},{3,19},{11,27},{19,3},{27,11},{5,21},{... | collective-permute-start | bytes 3145736 | tf_op jit(solution)/shard_map/ppermute | solution.py:545
  91.0 49.8 %collective-permute-start.21 = (f32[128,2048]{1,0:T(8,128)}, f32[128,2048]{1,0:T(8,128)}, u32[]{:S(2)}, u32[]{:S(2)}) collective-permute-start(f32[128,2048]{1,0:T(8,128)} %get-tuple-element.49), channel_id=1, source_target_pairs={{1,25},{9,1},{17,9},{25,17},{3,27},{11,3},{19,11},{27,19},{5,29},{... | collective-permute-start | bytes 3145736 | tf_op jit(solution)/shard_map/ppermute | solution.py:545
  92.6 48.2 %collective-permute-start.18 = (f32[4,128,512]{2,1,0:T(8,128)}, f32[4,128,512]{2,1,0:T(8,128)}, u32[]{:S(2)}, u32[]{:S(2)}) collective-permute-start(f32[4,128,512]{2,1,0:T(8,128)} %get-tuple-element.42.refs_5_), channel_id=1, source_target_pairs={{1,7},{3,5},{5,3},{7,1},{9,15},{11,13},{13,11},{15,9},{17,23},{19,... | collective-permute-start | bytes 3145736 | tf_op jit(solution)/shard_map/ppermute | solution.py:541
  94.3 46.5 %collective-permute-start.17 = (f32[4,128,512]{2,1,0:T(8,128)}, f32[4,128,512]{2,1,0:T(8,128)}, u32[]{:S(2)}, u32[]{:S(2)}) collective-permute-start(f32[4,128,512]{2,1,0:T(8,128)} %get-tuple-element.42.refs_5_), channel_id=1, source_target_pairs={{1,5},{3,7},{5,1},{7,3},{9,13},{11,15},{13,9},{15,11},{17,21},{19,... | collective-permute-start | bytes 3145736 | tf_op jit(solution)/shard_map/ppermute | solution.py:541
  95.9 44.9 %collective-permute-start.16 = (f32[4,128,512]{2,1,0:T(8,128)}, f32[4,128,512]{2,1,0:T(8,128)}, u32[]{:S(2)}, u32[]{:S(2)}) collective-permute-start(f32[4,128,512]{2,1,0:T(8,128)} %get-tuple-element.42.refs_5_), channel_id=1, source_target_pairs={{1,3},{3,1},{5,7},{7,5},{9,11},{11,9},{13,15},{15,13},{17,19},{19,... | collective-permute-start | bytes 3145736 | tf_op jit(solution)/shard_map/ppermute | solution.py:541
  142.8 33.5 %collective-permute-start.22 = (f32[768,1024]{1,0:T(8,128)}, f32[768,1024]{1,0:T(8,128)S(1)}, u32[]{:S(2)}, u32[]{:S(2)}) collective-permute-start(f32[768,1024]{1,0:T(8,128)} %pick.1.mine2), channel_id=1, source_target_pairs={{0,1},{1,0},{2,3},{3,2},{4,5},{5,4},{6,7},{7,6},{8,9},{9,8},{10,11... | collective-permute-start | bytes 9437192 | tf_op jit(solution)/shard_map/ppermute | solution.py:551
  (18 other events, 152.1 us)

commit v2 on v1

--- a/solution.py
+++ b/solution.py
@@ -169,7 +169,8 @@
         self.tiles = blocks_here // self.g
         self.windows = 2 * half // (rows * B) - self.npl
         self.pivot_first = 0 if self.npl == 2 else NB
-        self.n0 = rows + 1 if rows == 4 and self.windows % 2 == 0 else rows
+        self.pivot_cols = PW if self.npl == 2 else 0
+        self.gathers = rows + 1 if rows == 4 and self.windows % 2 == 0 else rows
         self.a_first = KP // B
         self.a_count = (half - KP) // B
         self.b_first = half // B
@@ -193,19 +194,19 @@
     return [lambda l, ref=ref: ref.at[l] for ref in whole] + [across]
 
 
-def route(z, info, dest, d):
+def route(z, info, d):
     front = lax.rem(info[3] + d, z.fronts)
     slot, place = jnp.int32(0), jnp.int32(-1)
     for k in range(z.kb):
-        hit = dest[k] == front
+        hit = info[4 + k] == front
         slot = jnp.where(hit, k, slot)
-        place = jnp.where(hit, dest[z.kb + k], place)
+        place = jnp.where(hit, info[4 + z.kb + k], place)
     return slot, place
 
 
-def read_places(z, blocks, places):
+def read_places(z, blocks, places, first=B):
     for d in range(z.fronts):
-        places[d] = jnp.max(blocks[d, B:EXT, :B]).astype(jnp.int32)
+        places[d] = jnp.max(blocks[d, first : first + EXT - B, :B]).astype(jnp.int32)
 
 
 def factor0_kernel(z, info, *refs):
@@ -227,7 +228,7 @@
     @pl.when(info[0] == 0)
     def _():
         copies = Copies(sems)
-        pick = lambda piece: [(0, piece.at[:, pl.ds(0, PW)])]
+        pick = lambda piece: [(0, piece.at[:, pl.ds(z.pivot_cols, PW)])]
         started = take_rows(copies, info[1], pieces, a_ref, z.pivot_first, NB, pick, slice(None))
         started.append(copies.start(i0_ref, f_s.at[:, pl.ds(0, PW)]))
         copies.wait(started)
@@ -241,7 +242,7 @@
     return [copies.start(packed.at[n, pl.ds(0, B)], f_s.at[pl.ds(n * B, B)]) for n in range(NB)]
 
 
-def sort_kernel(z, info, dest, first, second, *refs):
+def sort_kernel(z, info, first, second, *refs):
     f = z.fronts
     panel, late = refs[:f], refs[f : 2 * f]
     c_s, e_s, sems = refs[2 * f :]
@@ -250,7 +251,7 @@
     @pl.when(info[0] == 1)
     def _():
         copies = Copies(sems)
-        routes = [route(z, info, dest, d) for d in range(f)]
+        routes = [route(z, info, d) for d in range(f)]
         order = list(range(1, f)) + [0]
         reads = {}
         for d in order:
@@ -274,14 +275,14 @@
         copies.wait(writes)
 
 
-def window_kernel(z, info, other, _, *refs):
+def window_kernel(z, info, raw, _, *refs):
     f = z.fronts
-    panel, (h0, h1, back), (t_ref, c_ref, places, sems) = refs[:f], refs[f : f + 3], refs[f + 3 :]
+    panel, (window, back), (t_ref, c_ref, places, sems) = refs[:f], refs[f : f + 2], refs[f + 2 :]
 
     @pl.when(info[0] == 1)
     def _():
         copies = Copies(sems)
-        started = [copies.start(other.at[pl.ds(z.npl, z.windows), :, pl.ds(0, KP)], t_ref)]
+        started = [copies.start(raw, t_ref)]
         started += [copies.start(panel[d], c_ref.at[d]) for d in range(f)]
         copies.wait(started)
         later = [copies.start(c_ref, back)]
@@ -293,8 +294,7 @@
             def _():
                 t_ref[place] += c_ref[d, :B]
 
-        later.append(copies.start(t_ref.at[:, :, pl.ds(0, PW)], h0))
-        later.append(copies.start(t_ref.at[:, :, pl.ds(PW, PW)], h1))
+        later.append(copies.start(t_ref, window))
         copies.wait(later)
 
 
@@ -312,63 +312,84 @@
             t_ref[here, :] += blocks[d, :B]
 
 
-def both_kernel(z, info, mine, theirs, *refs):
-    pivots, w0, refs = refs[: z.rows], refs[z.rows : z.rows + z.n0], refs[z.rows + z.n0 :]
-    p_ref, x_ref, l_out, i_out, t_out, p_high, p_low, z_out = refs[:8]
-    a_ref, f_s, i_s, m_ref, u_ref, v_ref, w_s, t_s, c_s, inv, y, places, sems = refs[8:]
-    i = pl.program_id(0)
-
-    @pl.when((info[0] == 0) & (i == 0))
-    def _():
-        copies = Copies(sems)
-        pick = lambda piece: [(0, piece.at[:, pl.ds(PW, PW)])]
-        started = take_rows(copies, info[1], pivots, a_ref, z.pivot_first, NB, pick, slice(None))
+def factor1_kernel(z, info, mine, *refs):
+    pieces, (l_out, i_out, a_ref, f_s, m_ref, u_ref, v_ref, sems) = refs[: z.rows], refs[z.rows :]
+
+    @pl.when(info[0] == 0)
+    def _():
+        copies = Copies(sems)
+        pick = lambda piece: [(0, piece.at[:, pl.ds(z.pivot_cols + PW, PW)])]
+        started = take_rows(copies, info[1], pieces, a_ref, z.pivot_first, NB, pick, slice(None))
         started += take_factor(copies, mine, f_s)
         copies.wait(started)
         load_symmetric(a_ref, m_ref, 0)
         m_ref[:, :PW] = m_ref[:, :PW] - dot6(f_s[:, PW:], f_s[:, PW:], NT)
         panel_factor(m_ref, u_ref, v_ref)
-        store_factor(m_ref, l_out, i_s)
-        copies.wait([copies.start(i_s, i_out.at[pl.ds(0, PW), pl.ds(0, PW)])])
+        store_factor(m_ref, l_out, i_out)
+
+
+def panel_kernel(z, info, mine, theirs, p_ref, p_high, p_low, z_out, t_s, c_s, f_s, places, sems):
+    i = pl.program_id(0)
 
     @pl.when(info[0] == 1)
     def _():
         @pl.when(i == 0)
         def _():
             copies = Copies(sems)
-            used = z.window_blocks(z.b_first, z.b_count)
-            pick = lambda piece: [(l + z.npl, piece(l)) for l in used]
-            started = take_rows(copies, info[1], gathered(z, w0), w_s, z.b_first, z.b_count, pick, slice(None))
-            started += take_factor(copies, theirs, f_s)
+            started = take_factor(copies, theirs, f_s)
             started.append(copies.start(mine, c_s))
             copies.wait(started)
             read_places(z, c_s, places)
-            inv[0], inv[1] = split(f_s[:, :PW])
-            inverse = (inv[0], inv[1])
-            z_out[0], z_out[1] = split(dot3(split(f_s[:, PW:]), inverse, NN))
-            for n in range(z.half // PW):
-                span = slice(n * PW, (n + 1) * PW)
-                x = split(dot3(split(w_s[span, :]), inverse, NT))
-                y[0, span, :], y[1, span, :] = split(dot3(x, inverse, NN))
+            product = dot3(split(f_s[:, PW:]), split(f_s[:, :PW]), NN)
+            z_out[0], z_out[1] = split(product)
 
         fill_panel(z, info, places, c_s, i, p_ref, t_s)
         p = split(t_s[:, :PW])
-        high, low = split(t_s[:, PW:] - dot3(p, (z_out[0], z_out[1]), NT))
-        p_high[...] = high.reshape(p_high.shape)
-        p_low[...] = low.reshape(p_low.shape)
-        for n in range(z.half // PW):
-            span = slice(n * PW, (n + 1) * PW)
-            update = dot3(p, (y[0, span, :], y[1, span, :]), NT)
-            for l in range(z.g):
-                valid = ((i * z.g + l) * z.rows + info[1]) * B < info[2]
-                t_out[l, :, span] = (
-                    jnp.where(valid, x_ref[l, :, span], 0.0) - update[l * B : (l + 1) * B]
-                )
+        later = split(t_s[:, PW:] - dot3(p, (z_out[0], z_out[1]), NT))
+        for out, first, second in ((p_high, p[0], later[0]), (p_low, p[1], later[1])):
+            out[:, :, :PW] = first.reshape(z.g, B, PW)
+            out[:, :, PW:] = second.reshape(z.g, B, PW)
+
+
+def each_chunk(z, body):
+    def step(n, _):
+        body(pl.ds(pl.multiple_of(n * PW, PW), PW))
+        return 0
+
+    lax.fori_loop(0, z.half // PW, step, 0)
+
+
+def window_solve_kernel(z, info, theirs, z_ref, *refs):
+    w, refs = gathered(z, refs[: z.gathers]), refs[z.gathers :]
+    w_out, y_out, w_s, f_s, inv, y, sems = refs
+
+    @pl.when(info[0] == 1)
+    def _():
+        copies = Copies(sems)
+        used = z.window_blocks(z.b_first, z.b_count)
+        pick = lambda piece: [(l + z.npl, piece(l)) for l in used]
+        started = take_factor(copies, theirs, f_s)
+        started.append(copies.start(z_ref, inv.at[1]))
+        started += take_rows(copies, info[1], w, w_s, z.b_first, z.b_count, pick, slice(None))
+        copies.wait(started)
+        inv[0, 0], inv[0, 1] = split(f_s[:, :PW])
+
+        def project(span):
+            inverse = (inv[0, 0], inv[0, 1])
+            first = split(w_s[span, :PW])
+            x = split(dot3(first, inverse, NT))
+            y[0, span, :], y[1, span, :] = split(dot3(x, inverse, NN))
+            w_s[span, PW:] = w_s[span, PW:] - dot3(first, (inv[1, 0], inv[1, 1]), NT)
+
+        each_chunk(z, project)
+        copies.wait(
+            [copies.start(w_s.at[:, pl.ds(PW, PW)], w_out), copies.start(y, y_out)]
+        )
 
 
 def pick_kernel(z, info, *refs):
-    w0, w1, refs = refs[: z.n0], refs[z.n0 : z.n0 + z.rows], refs[z.n0 + z.rows :]
-    late, (_, out, w_s, sems) = refs[: z.fronts], refs[z.fronts :]
+    w, refs = gathered(z, refs[: z.gathers]), refs[z.gathers :]
+    late, (out, w_s, sems) = refs[: z.fronts], refs[z.fronts :]
     narrow = z.half - KP
 
     @pl.when(info[0] == 1)
@@ -376,24 +397,17 @@
         copies = Copies(sems)
         used = z.window_blocks(z.a_first, z.a_count)
         pick = lambda piece: [(l + z.npl, piece(l)) for l in used]
-        started = []
-        for n, pieces in enumerate((w0, w1)):
-            cols = pl.ds(n * PW, PW)
-            started += take_rows(
-                copies, info[1], gathered(z, pieces), w_s, z.a_first, z.a_count, pick, cols
-            )
+        started = take_rows(copies, info[1], w, w_s, z.a_first, z.a_count, pick, slice(None))
         for d in range(z.fronts):
             started.append(copies.start(late[d].at[:, pl.ds(0, narrow)], w_s.at[z.narrow_at(d)]))
         copies.wait(started)
         copies.wait([copies.start(w_s, out)])
 
 
-def final_kernel(z, info, mine, theirs, mine2, theirs2, l0_ref, l1_ref, z_ref, *refs):
+def final_kernel(z, info, mine, theirs, rest, i1_ref, i1r_ref, l0_ref, l1_ref, w_ref, y_ref, *refs):
     f = z.fronts
-    w0, w1, refs = refs[: z.n0], refs[z.n0 : z.n0 + z.rows], refs[z.n0 + z.rows :]
-    late, refs = refs[:f], refs[f:]
-    x_ref, t_ref, p_high, p_low, out = refs[:5]
-    t_s, c_s, w_s, e_s, i_s, s_s, inv, y, places, sems = refs[5:]
+    late, (x_ref, p_high, p_low, out), refs = refs[:f], refs[f : f + 4], refs[f + 4 :]
+    t_s, c_s, w_s, e_s, i_s, s_s, inv, y, places, sems = refs
     i = pl.program_id(0)
 
     def add_late(cols):
@@ -404,28 +418,33 @@
             def _():
                 out[at, :, cols] += e_s[d, :, cols]
 
+    def valid(l):
+        return ((i * z.g + l) * z.rows + info[1]) * B < info[2]
+
     @pl.when(info[0] == 0)
     def _():
         copies = Copies(sems)
-        right = pl.ds(KP, z.half - KP)
 
         @pl.when(i == 0)
         def _():
             started = [
-                copies.start(theirs2.at[pl.ds(0, PW), :], w_s.at[pl.ds(0, PW), :]),
-                copies.start(mine2.at[pl.ds(0, PW), pl.ds(0, PW)], i_s),
+                copies.start(rest.at[pl.ds(0, PW), pl.ds(0, PW)], w_s.at[0]),
+                copies.start(rest.at[pl.ds(0, PW), pl.ds(PW, PW)], w_s.at[1]),
+                copies.start(i1_ref, i_s),
                 copies.start(theirs, c_s),
             ]
             started += take_factor(copies, mine, s_s)
-            started += [copies.start(theirs2.at[z.narrow_at(d)], e_s.at[d, :, right]) for d in range(f)]
+            right = pl.ds(KP, z.half - KP)
+            arriving = [copies.start(rest.at[z.narrow_at(d)], e_s.at[d, :, right]) for d in range(f)]
             copies.wait(started)
             read_places(z, c_s, places)
             for n, value in enumerate((s_s[:, :PW], s_s[:, PW:], i_s[...])):
                 inv[n, 0], inv[n, 1] = split(value)
-            x = split(dot3(split(w_s[:PW, :PW]), (inv[0, 0], inv[0, 1]), NT))
+            x = split(dot3(split(w_s[0]), (inv[0, 0], inv[0, 1]), NT))
             inv[3, 0], inv[3, 1] = x
-            later = split(w_s[:PW, PW:] - dot3(x, (inv[1, 0], inv[1, 1]), NT))
+            later = split(w_s[1] - dot3(x, (inv[1, 0], inv[1, 1]), NT))
             inv[4, 0], inv[4, 1] = split(dot3(later, (inv[2, 0], inv[2, 1]), NT))
+            copies.wait(arriving)
 
         fill_panel(z, info, places, c_s, i, x_ref, t_s)
         x0 = dot3(split(t_s[:, :PW]), (inv[0, 0], inv[0, 1]), NT)
@@ -435,10 +454,9 @@
         update = dot3(x0s, (inv[3, 0], inv[3, 1]), NT) + dot3(split(x1), (inv[4, 0], inv[4, 1]), NT)
         for l in range(z.g):
             span = slice(l * B, (l + 1) * B)
-            valid = ((i * z.g + l) * z.rows + info[1]) * B < info[2]
             out[l, :, :PW] = x0[span]
             out[l, :, PW:KP] = x1[span]
-            out[l, :, KP:] = jnp.where(valid, x_ref[l, :, KP:], 0.0) - update[span]
+            out[l, :, KP:] = jnp.where(valid(l), x_ref[l, :, KP:], 0.0) - update[span]
         add_late(slice(KP, z.half))
 
         @pl.when(i == 0)
@@ -457,13 +475,10 @@
                 @pl.when(row >= PW)
                 def _():
                     here = pl.ds(pl.multiple_of(row - PW, B), B)
-                    piece = (row - PW) // B
-                    first = pltpu.make_async_copy(mine.at[piece, pl.ds(0, B), pl.ds(PW, PW)], out.at[l, :, pl.ds(0, PW)], sems.at[0])
-                    second = pltpu.make_async_copy(l1_ref.at[here], out.at[l, :, pl.ds(PW, PW)], sems.at[1])
-                    first.start()
-                    second.start()
-                    first.wait()
-                    second.wait()
+                    out[l, :, :PW] = s_s[here, PW:]
+                    copy = pltpu.make_async_copy(l1_ref.at[here], out.at[l, :, pl.ds(PW, PW)], sems.at[0])
+                    copy.start()
+                    copy.wait()
 
     @pl.when(info[0] == 1)
     def _():
@@ -471,35 +486,42 @@
 
         @pl.when(i == 0)
         def _():
-            used = z.window_blocks(z.b_first, z.b_count)
-            pick = lambda piece: [(l + z.npl, piece(l)) for l in used]
-            started = [copies.start(theirs2.at[pl.ds(0, PW), pl.ds(0, PW)], i_s)]
-            started.append(copies.start(z_ref, inv.at[1]))
-            started.append(copies.start(mine.at[:, pl.ds(B, EXT - B)], c_s.at[:, pl.ds(B, EXT - B)]))
-            for n, pieces in enumerate((w0, w1)):
-                cols = pl.ds(n * PW, PW)
-                started += take_rows(
-                    copies, info[1], gathered(z, pieces), w_s, z.b_first, z.b_count, pick, cols
-                )
+            started = [
+                copies.start(i1r_ref, i_s),
+                copies.start(mine.at[:, pl.ds(B, EXT - B)], c_s.at[:, pl.ds(B, EXT - B)]),
+            ]
+            for n in range(z.half // PW):
+                started.append(copies.start(w_ref.at[pl.ds(n * PW, PW)], w_s.at[n]))
+            arriving = [copies.start(y_ref, y.at[0])]
             right = pl.ds(z.half - KP, z.half)
-            arriving = [copies.start(late[d].at[:, right], e_s.at[d]) for d in range(f)]
+            arriving += [copies.start(late[d].at[:, right], e_s.at[d]) for d in range(f)]
             copies.wait(started)
             read_places(z, c_s, places)
-            inv[0, 0], inv[0, 1] = split(i_s[...])
-            inverse = (inv[0, 0], inv[0, 1])
-            for n in range(z.half // PW):
-                span = slice(n * PW, (n + 1) * PW)
-                w = w_s[span, PW:] - dot3(split(w_s[span, :PW]), (inv[1, 0], inv[1, 1]), NT)
-                x = split(dot3(split(w), inverse, NT))
-                y[0, span, :], y[1, span, :] = split(dot3(x, inverse, NN))
+            inverse = split(i_s[...])
+            inv[0, 0], inv[0, 1] = inverse
+
+            def project(n, _):
+                inverse = (inv[0, 0], inv[0, 1])
+                span = pl.ds(pl.multiple_of(n * PW, PW), PW)
+                x = split(dot3(split(w_s[n]), inverse, NT))
+                y[1, 0, span, :], y[1, 1, span, :] = split(dot3(x, inverse, NN))
+                return 0
+
+            lax.fori_loop(0, z.half // PW, project, 0)
             copies.wait(arriving)
 
-        p = (p_high[...].reshape(z.g * B, PW), p_low[...].reshape(z.g * B, PW))
+        p0 = tuple(p[:, :, :PW].reshape(z.g * B, PW) for p in (p_high, p_low))
+        p1 = tuple(p[:, :, PW:].reshape(z.g * B, PW) for p in (p_high, p_low))
+
+        def subtract(span):
+            update = dot3(p0, (y[0, 0, span, :], y[0, 1, span, :]), NT)
+            update = update + dot3(p1, (y[1, 0, span, :], y[1, 1, span, :]), NT)
+            for l in range(z.g):
+                present = jnp.where(valid(l), x_ref[l, :, span], 0.0)
+                out[l, :, span] = present - update[l * B : (l + 1) * B]
+
         for n in range(z.half // PW):
-            span = slice(n * PW, (n + 1) * PW)
-            update = dot3(p, (y[0, span, :], y[1, span, :]), NT)
-            for l in range(z.g):
-                out[l, :, span] = t_ref[l, :, span] - update[l * B : (l + 1) * B]
+            subtract(slice(n * PW, (n + 1) * PW))
         add_late(slice(0, z.half))
 
         @pl.when(i == 0)
@@ -512,6 +534,7 @@
 WHOLE = pl.BlockSpec(memory_space=pltpu.VMEM)
 SCALARS = pl.BlockSpec(memory_space=pltpu.SMEM)
 PARAMS = pltpu.CompilerParams(vmem_limit_bytes=VMEM_LIMIT)
+SHORT = pl.CostEstimate(flops=1, bytes_accessed=1, transcendentals=0)
 
 
 def shape(*dims, dtype=F32):
@@ -550,23 +573,25 @@
     def swap(x):
         return lax.ppermute(x, "col", [(0, 1), (1, 0)])
 
+    def from_other(x):
+        return lax.ppermute(x, "col", [(1, 0)])
+
     info = jnp.concatenate(
         [
             jnp.stack([col_here, row_here]).astype(jnp.int32),
             front_sizes,
             front_here.astype(jnp.int32)[None],
+            dest_front[0, :, 0],
+            dest_local[0, :, 0],
         ]
     )
-    dest = jnp.concatenate([dest_front[0, :, 0], dest_local[0, :, 0]])
-
-    q0 = matrix[0, :, :PW]
+    other_blocks = to_other(blocks)
+    pivot = matrix[z.npl - 1, :, :KP]
     if z.npl == 2:
-        pivot0 = from_rows(q0, 0)
-    other_blocks = to_other(blocks)
-    other = to_other(after(matrix, other_blocks))
-    pivot1 = from_rows(matrix[z.npl - 1, :, :KP], 0)
-    if z.npl != 2:
-        pivot0 = pivot1
+        pivot = jnp.concatenate([matrix[0, :, :PW], pivot], axis=1)
+    pivots = from_rows(pivot, 0)
+    raw = to_other(after(matrix, pivot)[z.npl : z.npl + z.windows, :, :KP])
+    other = to_other(after(matrix, other_blocks, *pivots, raw))
 
     factor_scratch = [
         pltpu.VMEM((PW, PW), F32),
@@ -581,8 +606,9 @@
         out_specs=[WHOLE] * 2,
         scratch_shapes=factor_scratch + [pltpu.SemaphoreType.DMA((rows,))],
         compiler_params=PARAMS,
+        cost_estimate=SHORT,
         name="factor0",
-    )(info, *pivot0)
+    )(info, *pivots)
     packed = pl.pallas_call(
         functools.partial(middle_kernel, z),
         out_shape=shape(fronts, EXT, KP),
@@ -594,13 +620,14 @@
             pltpu.SemaphoreType.DMA((rows + NB + 1,)),
         ],
         compiler_params=PARAMS,
+        cost_estimate=SHORT,
         name="middle",
-    )(info, i0, *pivot1)
+    )(info, i0, *pivots)
 
     refs = pl.pallas_call(
         functools.partial(sort_kernel, z),
         out_shape=[shape(EXT, KP)] * fronts + [shape(B, 2 * half - KP)] * fronts,
-        in_specs=[SCALARS] * 2 + [ANY] * 2,
+        in_specs=[SCALARS] + [ANY] * 2,
         out_specs=[ANY] * (2 * fronts),
         scratch_shapes=[
             pltpu.VMEM((fronts, EXT, KP), F32),
@@ -608,16 +635,17 @@
             pltpu.SemaphoreType.DMA((5 * fronts,)),
         ],
         compiler_params=PARAMS,
+        cost_estimate=SHORT,
         name="sort",
-    )(info, dest, after(other_blocks, packed), blocks)
+    )(info, other_blocks, blocks)
     panel, late = list(refs[:fronts]), list(refs[fronts:])
     panel = panel[:1] + [along_fronts(x, d + 1, 1, 1) for d, x in enumerate(panel[1:])]
-    h0, h1, mine = pl.pallas_call(
+    window, mine = pl.pallas_call(
         functools.partial(window_kernel, z),
-        out_shape=[shape(z.windows, B, PW)] * 2 + [shape(fronts, EXT, KP)],
+        out_shape=[shape(z.windows, B, KP), shape(fronts, EXT, KP)],
         in_specs=[SCALARS] + [ANY] * (fronts + 2),
-        out_specs=[ANY] * 3,
-        input_output_aliases={2: 2},
+        out_specs=[ANY] * 2,
+        input_output_aliases={2: 1},
         scratch_shapes=[
             pltpu.VMEM((z.windows, B, KP), F32),
             pltpu.VMEM((fronts, EXT, KP), F32),
@@ -625,70 +653,93 @@
             pltpu.SemaphoreType.DMA((fronts + 4,)),
         ],
         compiler_params=PARAMS,
+        cost_estimate=SHORT,
         name="window",
-    )(info, other, packed, *panel)
-    if z.n0 == rows:
-        w0 = from_rows(h0, 1)
+    )(info, raw, packed, *panel)
+    late = late[:1] + [along_fronts(after(x, window), d + 1, 1, 1) for d, x in enumerate(late[1:])]
+    if z.gathers == rows:
+        windows = from_rows(window, 1)
+        theirs = swap(mine)
     else:
         middle = z.windows // 2
-        sides = [along_rows(h0, 1, 1), along_rows(h0, 2, 1)]
-        across = [along_rows(sides[0][:middle], 2, 1), along_rows(sides[1][middle:], 1, 1)]
-        w0 = [h0, *sides, *across]
-    late = late[:1] + [along_fronts(after(x, h0), d + 1, 1, 1) for d, x in enumerate(late[1:])]
-    theirs = swap(after(mine, *w0))
-    w1 = from_rows(after(h1, *w0), 1)
-
-    def tile(width, core):
-        return pl.BlockSpec((z.g, B, width), lambda i, s: (jnp.where(s[0] == core, i, 0), 0, 0))
-
-    both = pltpu.VMEM((2, PW, PW), BF16)
-    rest = half - KP + -(-fronts * (half - KP) // KP) * B
-    l1, mine2, trailing, p_high, p_low, z_pair = pl.pallas_call(
-        functools.partial(both_kernel, z),
-        out_shape=[
-            shape(PW, PW),
-            shape(rest, KP),
-            shape(blocks_here, B, half),
-            shape(blocks_here, B, PW, dtype=BF16),
-            shape(blocks_here, B, PW, dtype=BF16),
-            shape(2, PW, PW, dtype=BF16),
-        ],
+        sides = [along_rows(window, 1, 1), along_rows(window, 2, 1)]
+        windows = [window, *sides]
+        theirs = swap(after(mine, *sides, late[1], late[-1]))
+        windows += [along_rows(sides[0][:middle], 2, 1), along_rows(sides[1][middle:], 1, 1)]
+
+    def tile(width, core, part=0):
+        return pl.BlockSpec((z.g, B, width), lambda i, s: (jnp.where(s[0] == core, i, 0), 0, part))
+
+    each = pl.BlockSpec((z.g, B, half), lambda i, s: (i, 0, 0))
+    pair = shape(blocks_here, B, KP, dtype=BF16)
+    p_high, p_low, z_pair = pl.pallas_call(
+        functools.partial(panel_kernel, z),
+        out_shape=[pair, pair, shape(2, PW, PW, dtype=BF16)],
         grid_spec=pltpu.PrefetchScalarGridSpec(
             num_scalar_prefetch=1,
             grid=(z.tiles,),
-            in_specs=[ANY] * (2 + rows + z.n0) + [tile(KP, 1), tile(half, 1)],
-            out_specs=[WHOLE, ANY, tile(half, 1), tile(PW, 1), tile(PW, 1), WHOLE],
-            scratch_shapes=factor_scratch[:1]
-            + [pltpu.VMEM((PW, 2 * PW), F32), pltpu.VMEM((PW, PW), F32)]
-            + factor_scratch[1:]
-            + [
-                pltpu.VMEM((half, PW), F32),
+            in_specs=[ANY] * 2 + [tile(KP, 1)],
+            out_specs=[tile(KP, 1), tile(KP, 1), WHOLE],
+            scratch_shapes=[
                 pltpu.VMEM((z.g * B, KP), F32),
                 pltpu.VMEM((fronts, EXT, KP), F32),
-                both,
-                pltpu.VMEM((2, half, PW), BF16),
+                pltpu.VMEM((PW, 2 * PW), F32),
                 pltpu.SMEM((fronts,), jnp.int32),
-                pltpu.SemaphoreType.DMA((rows * z.windows + NB + 2,)),
+                pltpu.SemaphoreType.DMA((NB + 1,)),
             ],
         ),
         compiler_params=PARAMS,
-        name="factor1_update0",
-    )(info, mine, theirs, *pivot1, *w0, other, matrix)
-
-    mine2 = pl.pallas_call(
+        cost_estimate=SHORT,
+        name="panel_rows",
+    )(info, mine, theirs, other)
+
+    l1, i1 = pl.pallas_call(
+        functools.partial(factor1_kernel, z),
+        out_shape=[shape(PW, PW)] * 2,
+        in_specs=[SCALARS] + [ANY] * (rows + 1),
+        out_specs=[WHOLE] * 2,
+        scratch_shapes=factor_scratch[:1]
+        + [pltpu.VMEM((PW, 2 * PW), F32)]
+        + factor_scratch[1:]
+        + [pltpu.SemaphoreType.DMA((rows + NB,))],
+        compiler_params=PARAMS,
+        cost_estimate=SHORT,
+        name="factor1",
+    )(info, after(mine, p_low), *pivots)
+    i1_other = to_other(i1)
+
+    w_next, y0 = pl.pallas_call(
+        functools.partial(window_solve_kernel, z),
+        out_shape=[shape(half, PW), shape(2, half, PW, dtype=BF16)],
+        in_specs=[SCALARS] + [ANY] * (2 + z.gathers),
+        out_specs=[ANY, ANY],
+        scratch_shapes=[
+            pltpu.VMEM((half, KP), F32),
+            pltpu.VMEM((PW, 2 * PW), F32),
+            pltpu.VMEM((2, 2, PW, PW), BF16),
+            pltpu.VMEM((2, half, PW), BF16),
+            pltpu.SemaphoreType.DMA((rows * z.windows + NB + 3,)),
+        ],
+        compiler_params=PARAMS,
+        cost_estimate=SHORT,
+        name="window_solve",
+    )(info, after(theirs, i1), z_pair, *windows)
+
+    rest_rows = half - KP + -(-fronts * (half - KP) // KP) * B
+    rest = pl.pallas_call(
         functools.partial(pick_kernel, z),
-        out_shape=shape(rest, KP),
-        in_specs=[SCALARS] + [ANY] * (z.n0 + rows + fronts + 1),
+        out_shape=shape(rest_rows, KP),
+        in_specs=[SCALARS] + [ANY] * (z.gathers + fronts),
         out_specs=ANY,
         scratch_shapes=[
-            pltpu.VMEM((rest, KP), F32),
-            pltpu.SemaphoreType.DMA((2 * rows * z.windows + fronts + 1,)),
+            pltpu.VMEM((rest_rows, KP), F32),
+            pltpu.SemaphoreType.DMA((rows * z.windows + fronts + 1,)),
         ],
-        input_output_aliases={1 + z.n0 + rows + fronts: 0},
-        compiler_params=PARAMS,
+        compiler_params=PARAMS,
+        cost_estimate=SHORT,
         name="pick",
-    )(info, *w0, *w1, *late, mine2)
-    theirs2 = swap(mine2)
+    )(info, *windows, *after(tuple(late), w_next))
+    rest = from_other(rest)
 
     out = pl.pallas_call(
         functools.partial(final_kernel, z),
@@ -696,25 +747,25 @@
         grid_spec=pltpu.PrefetchScalarGridSpec(
             num_scalar_prefetch=1,
             grid=(z.tiles,),
-            in_specs=[ANY] * (7 + z.n0 + rows + fronts)
-            + [tile(half, 0), tile(half, 1), tile(PW, 1), tile(PW, 1)],
-            out_specs=pl.BlockSpec((z.g, B, half), lambda i, s: (i, 0, 0)),
+            in_specs=[ANY] * (9 + fronts) + [each, tile(KP, 1), tile(KP, 1)],
+            out_specs=each,
             scratch_shapes=[
                 pltpu.VMEM((z.g * B, KP), F32),
                 pltpu.VMEM((fronts, EXT, KP), F32),
-                pltpu.VMEM((half, KP), F32),
+                pltpu.VMEM((half // PW, PW, PW), F32),
                 pltpu.VMEM((fronts, B, half), F32),
                 pltpu.VMEM((PW, PW), F32),
                 pltpu.VMEM((PW, 2 * PW), F32),
                 pltpu.VMEM((5, 2, PW, PW), BF16),
-                pltpu.VMEM((2, half, PW), BF16),
+                pltpu.VMEM((2, 2, half, PW), BF16),
                 pltpu.SMEM((fronts,), jnp.int32),
-                pltpu.SemaphoreType.DMA((2 * rows * z.windows + fronts + 8,)),
+                pltpu.SemaphoreType.DMA((2 * fronts + half // PW + NB + 4,)),
             ],
         ),
         compiler_params=PARAMS,
+        cost_estimate=SHORT,
         name="final",
-    )(info, mine, theirs, mine2, theirs2, l0, l1, z_pair, *w0, *w1, *late, matrix, trailing, p_high, p_low)
+    )(info, mine, theirs, rest, i1, i1_other, l0, l1, w_next, y0, *late, matrix, p_high, p_low)
     return out[None]
 
 

time: 224 us -> 200 us (0.89)
  the two profiles are of different devices: /device:TPU:0 before, /device:TPU:1 now
where the time goes in v2:
time: 200 us; the launch traced here: 199 us
  Pallas kernels  98.6 us (49%)
  starting transfers between devices  46.3 us (23%)
  waiting for transfers between devices  40.7 us (20%)
  local copies, waits for them, and re-layouts  12.1 us (6%)
    pallas_call x1, Pallas kernels, on_device(): pl.pallas_call(functools.partial(final_kernel, z), out_shape=shape(blocks...  45 us
    ppermute x6, waiting for transfers between devices, along_fronts(): return lax.ppermute(x, ('front', 'col'), pairs)  32.5 us
    ppermute x6, starting transfers between devices, along_fronts(): return lax.ppermute(x, ('front', 'col'), pairs)  26.8 us
    pallas_call x1, Pallas kernels, on_device(): pl.pallas_call(functools.partial(panel_kernel, z), out_shape=[pair, pair,...  17.7 us
    pallas_call x1, Pallas kernels, on_device(): pl.pallas_call(functools.partial(window_solve_kernel, z), out_shape=[shap...  15.3 us
    ppermute x7, starting transfers between devices, along_rows(): return lax.ppermute(x, ('row', 'col'), pairs)  12.7 us
    ppermute x4, waiting for transfers between devices, to_other(): return lax.ppermute(x, 'col', [(0, 1)])  7.39 us
    pallas_call x1, Pallas kernels, on_device(): pl.pallas_call(functools.partial(sort_kernel, z), out_shape=[shape(EXT, K...  6.23 us
  transfers between devices with their start and end apart: 19, of which 6 were waited for; matrix products, arithmetic and copies ran while one was open for 4% of the time, Pallas kernels for 25%

profile of v2, /device:TPU:1, one launch (start us, length us, event | category | flops | bytes accessed | tf_op | source)
XLA Modules:
  0.0 199.1 jit_solution(8347350539957871138)
XLA Ops:
  3.5 2.0 %slice.17 = f32[4,128,1024]{2,1,0:T(8,128)S(1)} slice(f32[24,128,1536]{2,1,0:T(8,128)} %bitcast.14), slice={[2:6], [0:128], [0:1024]} | slice | bytes 4194304 | tf_op jit(solution)/shard_map/slice | solution.py:593
  9.0 4.4 %collective-permute-done.raw = f32[4,128,1024]{2,1,0:T(8,128)} collective-permute-done((f32[4,128,1024]{2,1,0:T(8,128)S(1)}, f32[4,128,1024]{2,1,0:T(8,128)}, u32[]{:S(2)}, u32[]{:S(2)}) %collective-permute-start) | collective-permute-done | bytes 2097184 | tf_op jit(solution)/shard_map/ppermute | solution.py:571
  15.9 6.2 %sort.1 = (f32[136,1024]{1,0:T(8,128)}, f32[136,1024]{1,0:T(8,128)}, f32[136,1024]{1,0:T(8,128)}, f32[136,1024]{1,0:T(8,128)}, f32[128,2048]{1,0:T(8,128)}, /*in...) custom-call(s32[12]{0:T(128)} %concatenate.6.info, f32[4,128,1536]{2,1,0:T(8,128)} %collective-permute-done.4.first, ...), custom_call_target="tpu_custom_call" | custom-call | flops 1 | bytes 1 | tf_op jit(solution)/shard_map/sort/pallas_call | solution.py:627
  22.2 4.0 %collective-permute-start.5 = (f32[136,1024]{1,0:T(8,128)}, f32[136,1024]{1,0:T(8,128)S(1)}, u32[]{:S(2)}, u32[]{:S(2)}) collective-permute-start(f32[136,1024]{1,0:T(8,128)} %get-tuple-element.39), channel_id=1, source_target_pairs={{1,9},{9,17},{17,25},{25,1},{3,11},{11,19},{19,27},{27,3},{5,13},{... | collective-permute-start | bytes 1671176 | tf_op jit(solution)/shard_map/ppermute | solution.py:568
  26.2 4.2 %collective-permute-start.6 = (f32[136,1024]{1,0:T(8,128)}, f32[136,1024]{1,0:T(8,128)S(1)}, u32[]{:S(2)}, u32[]{:S(2)}) collective-permute-start(f32[136,1024]{1,0:T(8,128)} %get-tuple-element.40), channel_id=1, source_target_pairs={{1,17},{9,25},{17,1},{25,9},{3,19},{11,27},{19,3},{27,11},{5,21},{... | collective-permute-start | bytes 1671176 | tf_op jit(solution)/shard_map/ppermute | solution.py:568
  30.5 3.0 %collective-permute-start.7 = (f32[136,1024]{1,0:T(8,128)}, f32[136,1024]{1,0:T(8,128)S(1)}, u32[]{:S(2)}, u32[]{:S(2)}) collective-permute-start(f32[136,1024]{1,0:T(8,128)} %get-tuple-element.41), channel_id=1, source_target_pairs={{1,25},{9,1},{17,9},{25,17},{3,27},{11,3},{19,11},{27,19},{5,29},{... | collective-permute-start | bytes 1671176 | tf_op jit(solution)/shard_map/ppermute | solution.py:568
  33.4 2.0 %factor0.1 = (f32[512,512]{1,0:T(8,128)}, f32[512,512]{1,0:T(8,128)}) custom-call(s32[12]{0:T(128)} %concatenate.6.info, f32[128,1536]{1,0:T(8,128)} %copy-done.3, f32[128,1536]{1,0:T(8,128)} %copy-done.4, f32[128,1536]{1,0:T(8,128)} %copy-done.5, f32[128,1536]{1,0:T(8,128)} %copy-done.6), custom_call_target="tpu_custom_call" | custom-call | flops 1 | bytes 1 | tf_op jit(solution)/shard_map/factor0/pallas_call | solution.py:602
  36.3 11.1 %collective-permute-done.6.refs_2_ = f32[136,1024]{1,0:T(8,128)S(1)} collective-permute-done((f32[136,1024]{1,0:T(8,128)}, f32[136,1024]{1,0:T(8,128)S(1)}, u32[]{:S(2)}, u32[]{:S(2)}) %collective-permute-start.6) | collective-permute-done | bytes 557088 | tf_op jit(solution)/shard_map/ppermute | solution.py:568
  48.4 5.2 %window.1 = (f32[4,128,1024]{2,1,0:T(8,128)}, f32[4,136,1024]{2,1,0:T(8,128)}) custom-call(s32[12]{0:T(128)} %concatenate.6.info, f32[4,128,1024]{2,1,0:T(8,128)} %collective-permute-done.raw, f32[4,136,1024]{2,1,0:T(8,128)} %middle.1._, f32[136,1024]{1,0:T(8,128)} %get-tuple-element.38.refs_0_, ...), custom_call_target="tpu_custom_call", output_to_operand_aliasing={{1}: (2, {})} | custom-call | flops 1 | bytes 1 | tf_op jit(solution)/shard_map/window/pallas_call | solution.py:643
  53.6 3.1 %collective-permute-start.8 = (f32[4,128,1024]{2,1,0:T(8,128)}, f32[4,128,1024]{2,1,0:T(8,128)S(1)}, u32[]{:S(2)}, u32[]{:S(2)}) collective-permute-start(f32[4,128,1024]{2,1,0:T(8,128)} %get-tuple-element.43.refs_0_), channel_id=1, source_target_pairs={{1,3},{3,1},{5,7},{7,5},{9,11},{11,9},{13,15},{15,13},{17,19},{19,... | collective-permute-start | bytes 6291464 | tf_op jit(solution)/shard_map/ppermute | solution.py:564
  56.7 3.1 %collective-permute-start.9 = (f32[4,128,1024]{2,1,0:T(8,128)}, f32[4,128,1024]{2,1,0:T(8,128)S(1)}, u32[]{:S(2)}, u32[]{:S(2)}) collective-permute-start(f32[4,128,1024]{2,1,0:T(8,128)} %get-tuple-element.43.refs_0_), channel_id=1, source_target_pairs={{1,5},{3,7},{5,1},{7,3},{9,13},{11,15},{13,9},{15,11},{17,21},{19,... | collective-permute-start | bytes 6291464 | tf_op jit(solution)/shard_map/ppermute | solution.py:564
  59.9 9.2 %collective-permute-start.11 = (f32[128,2048]{1,0:T(8,128)S(1)}, f32[128,2048]{1,0:T(8,128)S(1)}, u32[]{:S(2)}, u32[]{:S(2)}) collective-permute-start(f32[128,2048]{1,0:T(8,128)S(1)} %copy-done.18), channel_id=1, source_target_pairs={{1,25},{9,1},{17,9},{25,17},{3,27},{11,3},{19,11},{27,19},{5,29},{... | collective-permute-start | bytes 3145736 | tf_op jit(solution)/shard_map/ppermute | solution.py:568
  69.1 1.9 collective-permute-start.10
  71.0 9.8 %collective-permute-done.11.refs_8_.refs_3_ = f32[128,2048]{1,0:T(8,128)S(1)} collective-permute-done((f32[128,2048]{1,0:T(8,128)S(1)}, f32[128,2048]{1,0:T(8,128)S(1)}, u32[]{:S(2)}, u32[]{:S(2)}) %collective-permute-start.11) | collective-permute-done | bytes 1048608 | tf_op jit(solution)/shard_map/ppermute | solution.py:568
  80.8 11.6 %collective-permute-done.10.refs_6_.refs_1_ = f32[128,2048]{1,0:T(8,128)S(1)} collective-permute-done((f32[128,2048]{1,0:T(8,128)S(1)}, f32[128,2048]{1,0:T(8,128)S(1)}, u32[]{:S(2)}, u32[]{:S(2)}) %collective-permute-start.10) | collective-permute-done | bytes 1048608 | tf_op jit(solution)/shard_map/ppermute | solution.py:568
  94.7 2.1 %collective-permute-start.13 = (f32[2,128,1024]{2,1,0:T(8,128)}, f32[2,128,1024]{2,1,0:T(8,128)}, u32[]{:S(2)}, u32[]{:S(2)}) collective-permute-start(f32[2,128,1024]{2,1,0:T(8,128)} %slice.22), channel_id=1, source_target_pairs={{1,5},{3,7},{5,1},{7,3},{9,13},{11,15},{13,9},{15,11},{17,21},{19,... | collective-permute-start | bytes 3145736 | tf_op jit(solution)/shard_map/ppermute | solution.py:564
  97.9 2.2 %collective-permute-start.14 = (f32[2,128,1024]{2,1,0:T(8,128)}, f32[2,128,1024]{2,1,0:T(8,128)}, u32[]{:S(2)}, u32[]{:S(2)}) collective-permute-start(f32[2,128,1024]{2,1,0:T(8,128)} %slice.23), channel_id=1, source_target_pairs={{1,3},{3,1},{5,7},{7,5},{9,11},{11,9},{13,15},{15,13},{17,19},{19,... | collective-permute-start | bytes 3145736 | tf_op jit(solution)/shard_map/ppermute | solution.py:564
  100.1 4.4 %collective-permute-start.15 = (f32[128,2048]{1,0:T(8,128)}, f32[128,2048]{1,0:T(8,128)}, u32[]{:S(2)}, u32[]{:S(2)}) collective-permute-start(f32[128,2048]{1,0:T(8,128)} %get-tuple-element.51), channel_id=1, source_target_pairs={{1,17},{9,25},{17,1},{25,9},{3,19},{11,27},{19,3},{27,11},{5,21},{... | collective-permute-start | bytes 3145736 | tf_op jit(solution)/shard_map/ppermute | solution.py:568
  105.9 17.7 %panel_rows.1 = (bf16[24,128,1024]{2,1,0:T(8,128)(2,1)}, bf16[24,128,1024]{2,1,0:T(8,128)(2,1)}, bf16[2,512,512]{2,1,0:T(8,128)(2,1)}) custom-call(s32[12]{0:T(128)} %concatenate.6.info, f32[4,136,1024]{2,1,0:T(8,128)} %get-tuple-element.54.mine, f32[4,136,1024]{2,1,0:T(8,128)} %copy-done, f32[24,128,1536]{2,1,0:T(8,128)} %collective-permute-done.16.p_ref), custom_call_target="tpu_custom_call" | custom-call | flops 1 | bytes 1 | tf_op jit(solution)/shard_map/panel_rows/pallas_call | solution.py:675
  123.6 2.1 %factor1.1 = (f32[512,512]{1,0:T(8,128)}, f32[512,512]{1,0:T(8,128)}) custom-call(s32[12]{0:T(128)} %concatenate.6.info, f32[4,136,1024]{2,1,0:T(8,128)} %get-tuple-element.54.mine, f32[128,1536]{1,0:T(8,128)} %copy-done.3, f32[128,1536]{1,0:T(8,128)} %copy-done.4, f32[128,1536]{1,0:T(8,128)} %copy-done.5, f32[128,1536]{1,0:T(8,128)} %copy-done.6), custom_call_target="tpu_custom_call" | custom-call | flops 1 | bytes 1 | tf_op jit(solution)/shard_map/factor1/pallas_call | solution.py:696
  125.7 15.3 %window_solve.1 = (f32[1536,512]{1,0:T(8,128)}, bf16[2,1536,512]{2,1,0:T(8,128)(2,1)}) custom-call(s32[12]{0:T(128)} %concatenate.6.info, f32[4,136,1024]{2,1,0:T(8,128)} %copy-done, bf16[2,512,512]{2,1,0:T(8,128)(2,1)} %get-tuple-element.57.z_ref, f32[4,128,1024]{2,1,0:T(8,128)} %get-tuple-element.43.refs_0_, f32[4,128,1024]{2,1,0:T(8,128)} %copy-done.1, ...), custom_call_target="tpu_custom_call" | custom-call | flops 1 | bytes 1 | tf_op jit(solution)/shard_map/window_solve/pallas_call | solution.py:711
  141.0 4.5 %pick.1 = f32[768,1024]{1,0:T(8,128)} custom-call(s32[12]{0:T(128)} %concatenate.6.info, f32[4,128,1024]{2,1,0:T(8,128)} %get-tuple-element.43.refs_0_, f32[4,128,1024]{2,1,0:T(8,128)} %copy-done.1, f32[4,128,1024]{2,1,0:T(8,128)} %copy-done.2, f32[2,128,1024]{2,1,0:T(8,128)} %collective-permute-done.13.refs_3_, ...), custom_call_target="tpu_custom_call" | custom-call | flops 1 | bytes 1 | tf_op jit(solution)/shard_map/pick/pallas_call | solution.py:729
  148.5 3.0 %collective-permute-done.18.i1r_ref = f32[512,512]{1,0:T(8,128)S(1)} collective-permute-done((f32[512,512]{1,0:T(8,128)S(1)}, f32[512,512]{1,0:T(8,128)S(1)}, u32[]{:S(2)}, u32[]{:S(2)}) %collective-permute-start.18) | collective-permute-done | bytes 1048608 | tf_op jit(solution)/shard_map/ppermute | solution.py:571
  154.0 45.0 %final.1 = f32[24,128,1536]{2,1,0:T(8,128)} custom-call(s32[12]{0:T(128)} %concatenate.6.info, f32[4,136,1024]{2,1,0:T(8,128)} %get-tuple-element.54.mine, f32[4,136,1024]{2,1,0:T(8,128)} %copy-done, f32[768,1024]{1,0:T(8,128)} %copy-done.9, f32[512,512]{1,0:T(8,128)} %get-tuple-element.55.i1_ref, f32[512,512]{1,0:T(8,128)} %copy-done.11, ...), custom_call_target="tpu_custom_call" | custom-call | flops 1 | bytes 1 | tf_op jit(solution)/shard_map/final/pallas_call | solution.py:744
  (68 shorter events, 20.7 us)
Async XLA Ops:
  0.0 13.3 %collective-permute-start.4 = (f32[4,128,1536]{2,1,0:T(8,128)}, f32[4,128,1536]{2,1,0:T(8,128)}, u32[]{:S(2)}, u32[]{:S(2)}) collective-permute-start(f32[4,128,1536]{2,1,0:T(8,128)} %bitcast.17), channel_id=1, source_target_pairs={{0,1},{2,3},{4,5},{6,7},{8,9},{10,11},{12,13},{14,15},{16,17},{18,... | collective-permute-start | bytes 9437192 | tf_op jit(solution)/shard_map/ppermute | solution.py:571
  3.4 18.7 %copy-start.3 = (f32[128,1536]{1,0:T(8,128)}, f32[128,1536]{1,0:T(8,128)S(1)}, u32[]{:S(2)}) copy-start(f32[128,1536]{1,0:T(8,128)S(1)} %pad_maximum_fusion.refs_0_) | copy-start | bytes 2359300
  5.5 7.9 %collective-permute-start = (f32[4,128,1024]{2,1,0:T(8,128)S(1)}, f32[4,128,1024]{2,1,0:T(8,128)}, u32[]{:S(2)}, u32[]{:S(2)}) collective-permute-start(f32[4,128,1024]{2,1,0:T(8,128)S(1)} %slice.17), channel_id=1, source_target_pairs={{0,1},{2,3},{4,5},{6,7},{8,9},{10,11},{12,13},{14,15},{16,17},{18,... | collective-permute-start | bytes 6291464 | tf_op jit(solution)/shard_map/ppermute | solution.py:571
  6.8 2.2 %collective-permute-start.1 = (f32[128,1536]{1,0:T(8,128)S(1)}, f32[128,1536]{1,0:T(8,128)S(1)}, u32[]{:S(2)}, u32[]{:S(2)}) collective-permute-start(f32[128,1536]{1,0:T(8,128)S(1)} %pad_maximum_fusion.refs_0_), channel_id=1, source_target_pairs={{0,2},{2,0},{4,6},{6,4},{8,10},{10,8},{12,14},{14,12},{16,18},{18,... | collective-permute-start | bytes 2359304 | tf_op jit(solution)/shard_map/ppermute | solution.py:564
  7.5 1.5 collective-permute-start.2
  8.2 0.8 collective-permute-start.3
  13.3 91.2 %collective-permute-start.16 = (f32[24,128,1536]{2,1,0:T(8,128)}, f32[24,128,1536]{2,1,0:T(8,128)}, u32[]{:S(2)}, u32[]{:S(2)}) collective-permute-start(f32[24,128,1536]{2,1,0:T(8,128)} %bitcast.15), channel_id=1, source_target_pairs={{0,1},{2,3},{4,5},{6,7},{8,9},{10,11},{12,13},{14,15},{16,17},{18,... | collective-permute-start | bytes 56623112 | tf_op jit(solution)/shard_map/ppermute | solution.py:571
  22.2 14.0 %collective-permute-start.5 = (f32[136,1024]{1,0:T(8,128)}, f32[136,1024]{1,0:T(8,128)S(1)}, u32[]{:S(2)}, u32[]{:S(2)}) collective-permute-start(f32[136,1024]{1,0:T(8,128)} %get-tuple-element.39), channel_id=1, source_target_pairs={{1,9},{9,17},{17,25},{25,1},{3,11},{11,19},{19,27},{27,3},{5,13},{... | collective-permute-start | bytes 1671176 | tf_op jit(solution)/shard_map/ppermute | solution.py:568
  26.2 21.1 %collective-permute-start.6 = (f32[136,1024]{1,0:T(8,128)}, f32[136,1024]{1,0:T(8,128)S(1)}, u32[]{:S(2)}, u32[]{:S(2)}) collective-permute-start(f32[136,1024]{1,0:T(8,128)} %get-tuple-element.40), channel_id=1, source_target_pairs={{1,17},{9,25},{17,1},{25,9},{3,19},{11,27},{19,3},{27,11},{5,21},{... | collective-permute-start | bytes 1671176 | tf_op jit(solution)/shard_map/ppermute | solution.py:568
  30.5 16.9 %collective-permute-start.7 = (f32[136,1024]{1,0:T(8,128)}, f32[136,1024]{1,0:T(8,128)S(1)}, u32[]{:S(2)}, u32[]{:S(2)}) collective-permute-start(f32[136,1024]{1,0:T(8,128)} %get-tuple-element.41), channel_id=1, source_target_pairs={{1,25},{9,1},{17,9},{25,17},{3,27},{11,3},{19,11},{27,19},{5,29},{... | collective-permute-start | bytes 1671176 | tf_op jit(solution)/shard_map/ppermute | solution.py:568
  48.4 20.7 %copy-start.17 = (f32[128,2048]{1,0:T(8,128)S(1)}, f32[128,2048]{1,0:T(8,128)}, u32[]{:S(2)}) copy-start(f32[128,2048]{1,0:T(8,128)} %get-tuple-element.45) | copy-start | bytes 3145732
  53.6 38.9 %collective-permute-start.8 = (f32[4,128,1024]{2,1,0:T(8,128)}, f32[4,128,1024]{2,1,0:T(8,128)S(1)}, u32[]{:S(2)}, u32[]{:S(2)}) collective-permute-start(f32[4,128,1024]{2,1,0:T(8,128)} %get-tuple-element.43.refs_0_), channel_id=1, source_target_pairs={{1,3},{3,1},{5,7},{7,5},{9,11},{11,9},{13,15},{15,13},{17,19},{19,... | collective-permute-start | bytes 6291464 | tf_op jit(solution)/shard_map/ppermute | solution.py:564
  56.7 35.8 %collective-permute-start.9 = (f32[4,128,1024]{2,1,0:T(8,128)}, f32[4,128,1024]{2,1,0:T(8,128)S(1)}, u32[]{:S(2)}, u32[]{:S(2)}) collective-permute-start(f32[4,128,1024]{2,1,0:T(8,128)} %get-tuple-element.43.refs_0_), channel_id=1, source_target_pairs={{1,5},{3,7},{5,1},{7,3},{9,13},{11,15},{13,9},{15,11},{17,21},{19,... | collective-permute-start | bytes 6291464 | tf_op jit(solution)/shard_map/ppermute | solution.py:564
  59.9 21.0 %collective-permute-start.11 = (f32[128,2048]{1,0:T(8,128)S(1)}, f32[128,2048]{1,0:T(8,128)S(1)}, u32[]{:S(2)}, u32[]{:S(2)}) collective-permute-start(f32[128,2048]{1,0:T(8,128)S(1)} %copy-done.18), channel_id=1, source_target_pairs={{1,25},{9,1},{17,9},{25,17},{3,27},{11,3},{19,11},{27,19},{5,29},{... | collective-permute-start | bytes 3145736 | tf_op jit(solution)/shard_map/ppermute | solution.py:568
  69.1 23.4 %collective-permute-start.10 = (f32[128,2048]{1,0:T(8,128)S(1)}, f32[128,2048]{1,0:T(8,128)S(1)}, u32[]{:S(2)}, u32[]{:S(2)}) collective-permute-start(f32[128,2048]{1,0:T(8,128)S(1)} %copy-done.17), channel_id=1, source_target_pairs={{1,9},{9,17},{17,25},{25,1},{3,11},{11,19},{19,27},{27,3},{5,13},{... | collective-permute-start | bytes 3145736 | tf_op jit(solution)/shard_map/ppermute | solution.py:568
  80.8 42.8 %copy-start.7 = (f32[128,2048]{1,0:T(8,128)}, f32[128,2048]{1,0:T(8,128)S(1)}, u32[]{:S(2)}) copy-start(f32[128,2048]{1,0:T(8,128)S(1)} %collective-permute-done.11.refs_8_.refs_3_) | copy-start | bytes 3145732
  92.5 31.1 %copy-start.1 = (f32[4,128,1024]{2,1,0:T(8,128)}, f32[4,128,1024]{2,1,0:T(8,128)S(1)}, u32[]{:S(2)}) copy-start(f32[4,128,1024]{2,1,0:T(8,128)S(1)} %collective-permute-done.8.refs_1_) | copy-start | bytes 6291460
  93.5 30.2 %copy-start.2 = (f32[4,128,1024]{2,1,0:T(8,128)}, f32[4,128,1024]{2,1,0:T(8,128)S(1)}, u32[]{:S(2)}) copy-start(f32[4,128,1024]{2,1,0:T(8,128)S(1)} %collective-permute-done.9.refs_2_) | copy-start | bytes 6291460
  93.5 11.1 %collective-permute-start.12 = (f32[4,136,1024]{2,1,0:T(8,128)}, f32[4,136,1024]{2,1,0:T(8,128)S(1)}, u32[]{:S(2)}, u32[]{:S(2)}) collective-permute-start(f32[4,136,1024]{2,1,0:T(8,128)} %get-tuple-element.54.mine), channel_id=1, source_target_pairs={{0,1},{1,0},{2,3},{3,2},{4,5},{5,4},{6,7},{7,6},{8,9},{9,8},{10,11... | collective-permute-start | bytes 6684680 | tf_op jit(solution)/shard_map/ppermute | solution.py:574
  94.7 31.0 %collective-permute-start.13 = (f32[2,128,1024]{2,1,0:T(8,128)}, f32[2,128,1024]{2,1,0:T(8,128)}, u32[]{:S(2)}, u32[]{:S(2)}) collective-permute-start(f32[2,128,1024]{2,1,0:T(8,128)} %slice.22), channel_id=1, source_target_pairs={{1,5},{3,7},{5,1},{7,3},{9,13},{11,15},{13,9},{15,11},{17,21},{19,... | collective-permute-start | bytes 3145736 | tf_op jit(solution)/shard_map/ppermute | solution.py:564
  97.9 27.8 %collective-permute-start.14 = (f32[2,128,1024]{2,1,0:T(8,128)}, f32[2,128,1024]{2,1,0:T(8,128)}, u32[]{:S(2)}, u32[]{:S(2)}) collective-permute-start(f32[2,128,1024]{2,1,0:T(8,128)} %slice.23), channel_id=1, source_target_pairs={{1,3},{3,1},{5,7},{7,5},{9,11},{11,9},{13,15},{15,13},{17,19},{19,... | collective-permute-start | bytes 3145736 | tf_op jit(solution)/shard_map/ppermute | solution.py:564
  100.1 40.9 %collective-permute-start.15 = (f32[128,2048]{1,0:T(8,128)}, f32[128,2048]{1,0:T(8,128)}, u32[]{:S(2)}, u32[]{:S(2)}) collective-permute-start(f32[128,2048]{1,0:T(8,128)} %get-tuple-element.51), channel_id=1, source_target_pairs={{1,17},{9,25},{17,1},{25,9},{3,19},{11,27},{19,3},{27,11},{5,21},{... | collective-permute-start | bytes 3145736 | tf_op jit(solution)/shard_map/ppermute | solution.py:568
  145.5 6.8 %collective-permute-start.17 = (f32[768,1024]{1,0:T(8,128)}, f32[768,1024]{1,0:T(8,128)S(1)}, u32[]{:S(2)}, u32[]{:S(2)}) collective-permute-start(f32[768,1024]{1,0:T(8,128)} %pick.1), channel_id=1, source_target_pairs={{1,0},{3,2},{5,4},{7,6},{9,8},{11,10},{13,12},{15,14},{17,16},{19,... | collective-permute-start | bytes 9437192 | tf_op jit(solution)/shard_map/ppermute | solution.py:577
  147.0 4.6 %collective-permute-start.18 = (f32[512,512]{1,0:T(8,128)S(1)}, f32[512,512]{1,0:T(8,128)S(1)}, u32[]{:S(2)}, u32[]{:S(2)}) collective-permute-start(f32[512,512]{1,0:T(8,128)S(1)} %copy-done.10), channel_id=1, source_target_pairs={{0,1},{2,3},{4,5},{6,7},{8,9},{10,11},{12,13},{14,15},{16,17},{18,... | collective-permute-start | bytes 3145736 | tf_op jit(solution)/shard_map/ppermute | solution.py:571
  (14 other events, 98.9 us)

commit v3 on v2

--- a/solution.py
+++ b/solution.py
@@ -374,17 +374,29 @@
         copies.wait(started)
         inv[0, 0], inv[0, 1] = split(f_s[:, :PW])
 
-        def project(span):
+        base = copies.count
+
+        def outgoing(n, span):
+            return [
+                pltpu.make_async_copy(y.at[:, span], y_out.at[:, span], sems.at[base + 2 * n]),
+                pltpu.make_async_copy(w_s.at[span, pl.ds(PW, PW)], w_out.at[span], sems.at[base + 2 * n + 1]),
+            ]
+
+        def project(n, _):
+            span = pl.ds(pl.multiple_of(n * PW, PW), PW)
             inverse = (inv[0, 0], inv[0, 1])
             first = split(w_s[span, :PW])
             x = split(dot3(first, inverse, NT))
             y[0, span, :], y[1, span, :] = split(dot3(x, inverse, NN))
             w_s[span, PW:] = w_s[span, PW:] - dot3(first, (inv[1, 0], inv[1, 1]), NT)
-
-        each_chunk(z, project)
-        copies.wait(
-            [copies.start(w_s.at[:, pl.ds(PW, PW)], w_out), copies.start(y, y_out)]
-        )
+            for copy in outgoing(n, span):
+                copy.start()
+            return 0
+
+        lax.fori_loop(0, z.half // PW, project, 0)
+        for n in range(z.half // PW):
+            for copy in outgoing(n, pl.ds(n * PW, PW)):
+                copy.wait()
 
 
 def pick_kernel(z, info, *refs):
@@ -718,7 +730,7 @@
             pltpu.VMEM((PW, 2 * PW), F32),
             pltpu.VMEM((2, 2, PW, PW), BF16),
             pltpu.VMEM((2, half, PW), BF16),
-            pltpu.SemaphoreType.DMA((rows * z.windows + NB + 3,)),
+            pltpu.SemaphoreType.DMA((rows * z.windows + NB + 2 * half // PW + 1,)),
         ],
         compiler_params=PARAMS,
         cost_estimate=SHORT,

time: 200 us -> 198 us (0.990)
  transfers between devices with their start and end apart: 19 -> 19, of which waited for: 6 -> 6; matrix products, arithmetic and copies ran while one was open for 4% -> 4% of each run, Pallas kernels for 25% -> 24%
where the time goes in v3:
time: 198 us
  Pallas kernels  97.1 us (49%)
  starting transfers between devices  46.3 us (23%)
  waiting for transfers between devices  40.7 us (21%)
  local copies, waits for them, and re-layouts  12.1 us (6%)
    pallas_call x1, Pallas kernels, on_device(): pl.pallas_call(functools.partial(final_kernel, z), out_shape=shape(blocks...  45 us
    ppermute x6, waiting for transfers between devices, along_fronts(): return lax.ppermute(x, ('front', 'col'), pairs)  32.5 us
    ppermute x6, starting transfers between devices, along_fronts(): return lax.ppermute(x, ('front', 'col'), pairs)  26.8 us
    pallas_call x1, Pallas kernels, on_device(): pl.pallas_call(functools.partial(panel_kernel, z), out_shape=[pair, pair,...  17.7 us
    pallas_call x1, Pallas kernels, on_device(): pl.pallas_call(functools.partial(window_solve_kernel, z), out_shape=[shap...  13.6 us
    ppermute x7, starting transfers between devices, along_rows(): return lax.ppermute(x, ('row', 'col'), pairs)  12.7 us
    ppermute x4, waiting for transfers between devices, to_other(): return lax.ppermute(x, 'col', [(0, 1)])  7.39 us
    pallas_call x1, Pallas kernels, on_device(): pl.pallas_call(functools.partial(sort_kernel, z), out_shape=[shape(EXT, K...  6.23 us
  transfers between devices with their start and end apart: 19, of which 6 were waited for; matrix products, arithmetic and copies ran while one was open for 4% of the time, Pallas kernels for 24%

profile of v3, /device:TPU:1, one launch (start us, length us, event | category | flops | bytes accessed | tf_op | source)
XLA Modules:
  0.0 197.6 jit_solution(2952253427886047872)
XLA Ops:
  3.5 2.0 %slice.17 = f32[4,128,1024]{2,1,0:T(8,128)S(1)} slice(f32[24,128,1536]{2,1,0:T(8,128)} %bitcast.14), slice={[2:6], [0:128], [0:1024]} | slice | bytes 4194304 | tf_op jit(solution)/shard_map/slice | solution.py:605
  9.0 4.4 %collective-permute-done.raw = f32[4,128,1024]{2,1,0:T(8,128)} collective-permute-done((f32[4,128,1024]{2,1,0:T(8,128)S(1)}, f32[4,128,1024]{2,1,0:T(8,128)}, u32[]{:S(2)}, u32[]{:S(2)}) %collective-permute-start) | collective-permute-done | bytes 2097184 | tf_op jit(solution)/shard_map/ppermute | solution.py:583
  15.9 6.2 %sort.1 = (f32[136,1024]{1,0:T(8,128)}, f32[136,1024]{1,0:T(8,128)}, f32[136,1024]{1,0:T(8,128)}, f32[136,1024]{1,0:T(8,128)}, f32[128,2048]{1,0:T(8,128)}, /*in...) custom-call(s32[12]{0:T(128)} %concatenate.6.info, f32[4,128,1536]{2,1,0:T(8,128)} %collective-permute-done.4.first, ...), custom_call_target="tpu_custom_call" | custom-call | flops 1 | bytes 1 | tf_op jit(solution)/shard_map/sort/pallas_call | solution.py:639
  22.2 4.0 %collective-permute-start.5 = (f32[136,1024]{1,0:T(8,128)}, f32[136,1024]{1,0:T(8,128)S(1)}, u32[]{:S(2)}, u32[]{:S(2)}) collective-permute-start(f32[136,1024]{1,0:T(8,128)} %get-tuple-element.39), channel_id=1, source_target_pairs={{1,9},{9,17},{17,25},{25,1},{3,11},{11,19},{19,27},{27,3},{5,13},{... | collective-permute-start | bytes 1671176 | tf_op jit(solution)/shard_map/ppermute | solution.py:580
  26.2 4.2 %collective-permute-start.6 = (f32[136,1024]{1,0:T(8,128)}, f32[136,1024]{1,0:T(8,128)S(1)}, u32[]{:S(2)}, u32[]{:S(2)}) collective-permute-start(f32[136,1024]{1,0:T(8,128)} %get-tuple-element.40), channel_id=1, source_target_pairs={{1,17},{9,25},{17,1},{25,9},{3,19},{11,27},{19,3},{27,11},{5,21},{... | collective-permute-start | bytes 1671176 | tf_op jit(solution)/shard_map/ppermute | solution.py:580
  30.5 3.0 %collective-permute-start.7 = (f32[136,1024]{1,0:T(8,128)}, f32[136,1024]{1,0:T(8,128)S(1)}, u32[]{:S(2)}, u32[]{:S(2)}) collective-permute-start(f32[136,1024]{1,0:T(8,128)} %get-tuple-element.41), channel_id=1, source_target_pairs={{1,25},{9,1},{17,9},{25,17},{3,27},{11,3},{19,11},{27,19},{5,29},{... | collective-permute-start | bytes 1671176 | tf_op jit(solution)/shard_map/ppermute | solution.py:580
  33.4 2.0 %factor0.1 = (f32[512,512]{1,0:T(8,128)}, f32[512,512]{1,0:T(8,128)}) custom-call(s32[12]{0:T(128)} %concatenate.6.info, f32[128,1536]{1,0:T(8,128)} %copy-done.3, f32[128,1536]{1,0:T(8,128)} %copy-done.4, f32[128,1536]{1,0:T(8,128)} %copy-done.5, f32[128,1536]{1,0:T(8,128)} %copy-done.6), custom_call_target="tpu_custom_call" | custom-call | flops 1 | bytes 1 | tf_op jit(solution)/shard_map/factor0/pallas_call | solution.py:614
  36.3 11.1 %collective-permute-done.6.refs_2_ = f32[136,1024]{1,0:T(8,128)S(1)} collective-permute-done((f32[136,1024]{1,0:T(8,128)}, f32[136,1024]{1,0:T(8,128)S(1)}, u32[]{:S(2)}, u32[]{:S(2)}) %collective-permute-start.6) | collective-permute-done | bytes 557088 | tf_op jit(solution)/shard_map/ppermute | solution.py:580
  48.4 5.2 %window.1 = (f32[4,128,1024]{2,1,0:T(8,128)}, f32[4,136,1024]{2,1,0:T(8,128)}) custom-call(s32[12]{0:T(128)} %concatenate.6.info, f32[4,128,1024]{2,1,0:T(8,128)} %collective-permute-done.raw, f32[4,136,1024]{2,1,0:T(8,128)} %middle.1._, f32[136,1024]{1,0:T(8,128)} %get-tuple-element.38.refs_0_, ...), custom_call_target="tpu_custom_call", output_to_operand_aliasing={{1}: (2, {})} | custom-call | flops 1 | bytes 1 | tf_op jit(solution)/shard_map/window/pallas_call | solution.py:655
  53.6 3.1 %collective-permute-start.8 = (f32[4,128,1024]{2,1,0:T(8,128)}, f32[4,128,1024]{2,1,0:T(8,128)S(1)}, u32[]{:S(2)}, u32[]{:S(2)}) collective-permute-start(f32[4,128,1024]{2,1,0:T(8,128)} %get-tuple-element.43.refs_0_), channel_id=1, source_target_pairs={{1,3},{3,1},{5,7},{7,5},{9,11},{11,9},{13,15},{15,13},{17,19},{19,... | collective-permute-start | bytes 6291464 | tf_op jit(solution)/shard_map/ppermute | solution.py:576
  56.7 3.1 %collective-permute-start.9 = (f32[4,128,1024]{2,1,0:T(8,128)}, f32[4,128,1024]{2,1,0:T(8,128)S(1)}, u32[]{:S(2)}, u32[]{:S(2)}) collective-permute-start(f32[4,128,1024]{2,1,0:T(8,128)} %get-tuple-element.43.refs_0_), channel_id=1, source_target_pairs={{1,5},{3,7},{5,1},{7,3},{9,13},{11,15},{13,9},{15,11},{17,21},{19,... | collective-permute-start | bytes 6291464 | tf_op jit(solution)/shard_map/ppermute | solution.py:576
  59.9 9.2 %collective-permute-start.11 = (f32[128,2048]{1,0:T(8,128)S(1)}, f32[128,2048]{1,0:T(8,128)S(1)}, u32[]{:S(2)}, u32[]{:S(2)}) collective-permute-start(f32[128,2048]{1,0:T(8,128)S(1)} %copy-done.18), channel_id=1, source_target_pairs={{1,25},{9,1},{17,9},{25,17},{3,27},{11,3},{19,11},{27,19},{5,29},{... | collective-permute-start | bytes 3145736 | tf_op jit(solution)/shard_map/ppermute | solution.py:580
  69.1 1.9 collective-permute-start.10
  71.0 9.8 %collective-permute-done.11.refs_8_.refs_3_ = f32[128,2048]{1,0:T(8,128)S(1)} collective-permute-done((f32[128,2048]{1,0:T(8,128)S(1)}, f32[128,2048]{1,0:T(8,128)S(1)}, u32[]{:S(2)}, u32[]{:S(2)}) %collective-permute-start.11) | collective-permute-done | bytes 1048608 | tf_op jit(solution)/shard_map/ppermute | solution.py:580
  80.8 11.6 %collective-permute-done.10.refs_6_.refs_1_ = f32[128,2048]{1,0:T(8,128)S(1)} collective-permute-done((f32[128,2048]{1,0:T(8,128)S(1)}, f32[128,2048]{1,0:T(8,128)S(1)}, u32[]{:S(2)}, u32[]{:S(2)}) %collective-permute-start.10) | collective-permute-done | bytes 1048608 | tf_op jit(solution)/shard_map/ppermute | solution.py:580
  94.7 2.1 %collective-permute-start.13 = (f32[2,128,1024]{2,1,0:T(8,128)}, f32[2,128,1024]{2,1,0:T(8,128)}, u32[]{:S(2)}, u32[]{:S(2)}) collective-permute-start(f32[2,128,1024]{2,1,0:T(8,128)} %slice.22), channel_id=1, source_target_pairs={{1,5},{3,7},{5,1},{7,3},{9,13},{11,15},{13,9},{15,11},{17,21},{19,... | collective-permute-start | bytes 3145736 | tf_op jit(solution)/shard_map/ppermute | solution.py:576
  97.9 2.2 %collective-permute-start.14 = (f32[2,128,1024]{2,1,0:T(8,128)}, f32[2,128,1024]{2,1,0:T(8,128)}, u32[]{:S(2)}, u32[]{:S(2)}) collective-permute-start(f32[2,128,1024]{2,1,0:T(8,128)} %slice.23), channel_id=1, source_target_pairs={{1,3},{3,1},{5,7},{7,5},{9,11},{11,9},{13,15},{15,13},{17,19},{19,... | collective-permute-start | bytes 3145736 | tf_op jit(solution)/shard_map/ppermute | solution.py:576
  100.1 4.4 %collective-permute-start.15 = (f32[128,2048]{1,0:T(8,128)}, f32[128,2048]{1,0:T(8,128)}, u32[]{:S(2)}, u32[]{:S(2)}) collective-permute-start(f32[128,2048]{1,0:T(8,128)} %get-tuple-element.51), channel_id=1, source_target_pairs={{1,17},{9,25},{17,1},{25,9},{3,19},{11,27},{19,3},{27,11},{5,21},{... | collective-permute-start | bytes 3145736 | tf_op jit(solution)/shard_map/ppermute | solution.py:580
  105.9 17.7 %panel_rows.1 = (bf16[24,128,1024]{2,1,0:T(8,128)(2,1)}, bf16[24,128,1024]{2,1,0:T(8,128)(2,1)}, bf16[2,512,512]{2,1,0:T(8,128)(2,1)}) custom-call(s32[12]{0:T(128)} %concatenate.6.info, f32[4,136,1024]{2,1,0:T(8,128)} %get-tuple-element.54.mine, f32[4,136,1024]{2,1,0:T(8,128)} %copy-done, f32[24,128,1536]{2,1,0:T(8,128)} %collective-permute-done.16.p_ref), custom_call_target="tpu_custom_call" | custom-call | flops 1 | bytes 1 | tf_op jit(solution)/shard_map/panel_rows/pallas_call | solution.py:687
  123.7 2.1 %factor1.1 = (f32[512,512]{1,0:T(8,128)}, f32[512,512]{1,0:T(8,128)}) custom-call(s32[12]{0:T(128)} %concatenate.6.info, f32[4,136,1024]{2,1,0:T(8,128)} %get-tuple-element.54.mine, f32[128,1536]{1,0:T(8,128)} %copy-done.3, f32[128,1536]{1,0:T(8,128)} %copy-done.4, f32[128,1536]{1,0:T(8,128)} %copy-done.5, f32[128,1536]{1,0:T(8,128)} %copy-done.6), custom_call_target="tpu_custom_call" | custom-call | flops 1 | bytes 1 | tf_op jit(solution)/shard_map/factor1/pallas_call | solution.py:708
  125.8 13.6 %window_solve.1 = (f32[1536,512]{1,0:T(8,128)}, bf16[2,1536,512]{2,1,0:T(8,128)(2,1)}) custom-call(s32[12]{0:T(128)} %concatenate.6.info, f32[4,136,1024]{2,1,0:T(8,128)} %copy-done, bf16[2,512,512]{2,1,0:T(8,128)(2,1)} %get-tuple-element.57.z_ref, f32[4,128,1024]{2,1,0:T(8,128)} %get-tuple-element.43.refs_0_, f32[4,128,1024]{2,1,0:T(8,128)} %copy-done.1, ...), custom_call_target="tpu_custom_call" | custom-call | flops 1 | bytes 1 | tf_op jit(solution)/shard_map/window_solve/pallas_call | solution.py:723
  139.5 4.5 %pick.1 = f32[768,1024]{1,0:T(8,128)} custom-call(s32[12]{0:T(128)} %concatenate.6.info, f32[4,128,1024]{2,1,0:T(8,128)} %get-tuple-element.43.refs_0_, f32[4,128,1024]{2,1,0:T(8,128)} %copy-done.1, f32[4,128,1024]{2,1,0:T(8,128)} %copy-done.2, f32[2,128,1024]{2,1,0:T(8,128)} %collective-permute-done.13.refs_3_, ...), custom_call_target="tpu_custom_call" | custom-call | flops 1 | bytes 1 | tf_op jit(solution)/shard_map/pick/pallas_call | solution.py:741
  147.0 3.0 %collective-permute-done.18.i1r_ref = f32[512,512]{1,0:T(8,128)S(1)} collective-permute-done((f32[512,512]{1,0:T(8,128)S(1)}, f32[512,512]{1,0:T(8,128)S(1)}, u32[]{:S(2)}, u32[]{:S(2)}) %collective-permute-start.18) | collective-permute-done | bytes 1048608 | tf_op jit(solution)/shard_map/ppermute | solution.py:583
  152.4 45.0 %final.1 = f32[24,128,1536]{2,1,0:T(8,128)} custom-call(s32[12]{0:T(128)} %concatenate.6.info, f32[4,136,1024]{2,1,0:T(8,128)} %get-tuple-element.54.mine, f32[4,136,1024]{2,1,0:T(8,128)} %copy-done, f32[768,1024]{1,0:T(8,128)} %copy-done.9, f32[512,512]{1,0:T(8,128)} %get-tuple-element.55.i1_ref, f32[512,512]{1,0:T(8,128)} %copy-done.11, ...), custom_call_target="tpu_custom_call" | custom-call | flops 1 | bytes 1 | tf_op jit(solution)/shard_map/final/pallas_call | solution.py:756
  (68 shorter events, 20.7 us)
Async XLA Ops:
  0.0 13.3 %collective-permute-start.4 = (f32[4,128,1536]{2,1,0:T(8,128)}, f32[4,128,1536]{2,1,0:T(8,128)}, u32[]{:S(2)}, u32[]{:S(2)}) collective-permute-start(f32[4,128,1536]{2,1,0:T(8,128)} %bitcast.17), channel_id=1, source_target_pairs={{0,1},{2,3},{4,5},{6,7},{8,9},{10,11},{12,13},{14,15},{16,17},{18,... | collective-permute-start | bytes 9437192 | tf_op jit(solution)/shard_map/ppermute | solution.py:583
  3.4 18.7 %copy-start.3 = (f32[128,1536]{1,0:T(8,128)}, f32[128,1536]{1,0:T(8,128)S(1)}, u32[]{:S(2)}) copy-start(f32[128,1536]{1,0:T(8,128)S(1)} %pad_maximum_fusion.refs_0_) | copy-start | bytes 2359300
  5.5 7.9 %collective-permute-start = (f32[4,128,1024]{2,1,0:T(8,128)S(1)}, f32[4,128,1024]{2,1,0:T(8,128)}, u32[]{:S(2)}, u32[]{:S(2)}) collective-permute-start(f32[4,128,1024]{2,1,0:T(8,128)S(1)} %slice.17), channel_id=1, source_target_pairs={{0,1},{2,3},{4,5},{6,7},{8,9},{10,11},{12,13},{14,15},{16,17},{18,... | collective-permute-start | bytes 6291464 | tf_op jit(solution)/shard_map/ppermute | solution.py:583
  6.8 2.2 %collective-permute-start.1 = (f32[128,1536]{1,0:T(8,128)S(1)}, f32[128,1536]{1,0:T(8,128)S(1)}, u32[]{:S(2)}, u32[]{:S(2)}) collective-permute-start(f32[128,1536]{1,0:T(8,128)S(1)} %pad_maximum_fusion.refs_0_), channel_id=1, source_target_pairs={{0,2},{2,0},{4,6},{6,4},{8,10},{10,8},{12,14},{14,12},{16,18},{18,... | collective-permute-start | bytes 2359304 | tf_op jit(solution)/shard_map/ppermute | solution.py:576
  7.5 1.5 collective-permute-start.2
  8.2 0.8 collective-permute-start.3
  13.3 91.2 %collective-permute-start.16 = (f32[24,128,1536]{2,1,0:T(8,128)}, f32[24,128,1536]{2,1,0:T(8,128)}, u32[]{:S(2)}, u32[]{:S(2)}) collective-permute-start(f32[24,128,1536]{2,1,0:T(8,128)} %bitcast.15), channel_id=1, source_target_pairs={{0,1},{2,3},{4,5},{6,7},{8,9},{10,11},{12,13},{14,15},{16,17},{18,... | collective-permute-start | bytes 56623112 | tf_op jit(solution)/shard_map/ppermute | solution.py:583
  22.2 14.0 %collective-permute-start.5 = (f32[136,1024]{1,0:T(8,128)}, f32[136,1024]{1,0:T(8,128)S(1)}, u32[]{:S(2)}, u32[]{:S(2)}) collective-permute-start(f32[136,1024]{1,0:T(8,128)} %get-tuple-element.39), channel_id=1, source_target_pairs={{1,9},{9,17},{17,25},{25,1},{3,11},{11,19},{19,27},{27,3},{5,13},{... | collective-permute-start | bytes 1671176 | tf_op jit(solution)/shard_map/ppermute | solution.py:580
  26.2 21.1 %collective-permute-start.6 = (f32[136,1024]{1,0:T(8,128)}, f32[136,1024]{1,0:T(8,128)S(1)}, u32[]{:S(2)}, u32[]{:S(2)}) collective-permute-start(f32[136,1024]{1,0:T(8,128)} %get-tuple-element.40), channel_id=1, source_target_pairs={{1,17},{9,25},{17,1},{25,9},{3,19},{11,27},{19,3},{27,11},{5,21},{... | collective-permute-start | bytes 1671176 | tf_op jit(solution)/shard_map/ppermute | solution.py:580
  30.5 16.9 %collective-permute-start.7 = (f32[136,1024]{1,0:T(8,128)}, f32[136,1024]{1,0:T(8,128)S(1)}, u32[]{:S(2)}, u32[]{:S(2)}) collective-permute-start(f32[136,1024]{1,0:T(8,128)} %get-tuple-element.41), channel_id=1, source_target_pairs={{1,25},{9,1},{17,9},{25,17},{3,27},{11,3},{19,11},{27,19},{5,29},{... | collective-permute-start | bytes 1671176 | tf_op jit(solution)/shard_map/ppermute | solution.py:580
  48.4 20.7 %copy-start.17 = (f32[128,2048]{1,0:T(8,128)S(1)}, f32[128,2048]{1,0:T(8,128)}, u32[]{:S(2)}) copy-start(f32[128,2048]{1,0:T(8,128)} %get-tuple-element.45) | copy-start | bytes 3145732
  53.6 38.9 %collective-permute-start.8 = (f32[4,128,1024]{2,1,0:T(8,128)}, f32[4,128,1024]{2,1,0:T(8,128)S(1)}, u32[]{:S(2)}, u32[]{:S(2)}) collective-permute-start(f32[4,128,1024]{2,1,0:T(8,128)} %get-tuple-element.43.refs_0_), channel_id=1, source_target_pairs={{1,3},{3,1},{5,7},{7,5},{9,11},{11,9},{13,15},{15,13},{17,19},{19,... | collective-permute-start | bytes 6291464 | tf_op jit(solution)/shard_map/ppermute | solution.py:576
  56.7 35.8 %collective-permute-start.9 = (f32[4,128,1024]{2,1,0:T(8,128)}, f32[4,128,1024]{2,1,0:T(8,128)S(1)}, u32[]{:S(2)}, u32[]{:S(2)}) collective-permute-start(f32[4,128,1024]{2,1,0:T(8,128)} %get-tuple-element.43.refs_0_), channel_id=1, source_target_pairs={{1,5},{3,7},{5,1},{7,3},{9,13},{11,15},{13,9},{15,11},{17,21},{19,... | collective-permute-start | bytes 6291464 | tf_op jit(solution)/shard_map/ppermute | solution.py:576
  59.9 21.0 %collective-permute-start.11 = (f32[128,2048]{1,0:T(8,128)S(1)}, f32[128,2048]{1,0:T(8,128)S(1)}, u32[]{:S(2)}, u32[]{:S(2)}) collective-permute-start(f32[128,2048]{1,0:T(8,128)S(1)} %copy-done.18), channel_id=1, source_target_pairs={{1,25},{9,1},{17,9},{25,17},{3,27},{11,3},{19,11},{27,19},{5,29},{... | collective-permute-start | bytes 3145736 | tf_op jit(solution)/shard_map/ppermute | solution.py:580
  69.1 23.4 %collective-permute-start.10 = (f32[128,2048]{1,0:T(8,128)S(1)}, f32[128,2048]{1,0:T(8,128)S(1)}, u32[]{:S(2)}, u32[]{:S(2)}) collective-permute-start(f32[128,2048]{1,0:T(8,128)S(1)} %copy-done.17), channel_id=1, source_target_pairs={{1,9},{9,17},{17,25},{25,1},{3,11},{11,19},{19,27},{27,3},{5,13},{... | collective-permute-start | bytes 3145736 | tf_op jit(solution)/shard_map/ppermute | solution.py:580
  80.8 42.8 %copy-start.7 = (f32[128,2048]{1,0:T(8,128)}, f32[128,2048]{1,0:T(8,128)S(1)}, u32[]{:S(2)}) copy-start(f32[128,2048]{1,0:T(8,128)S(1)} %collective-permute-done.11.refs_8_.refs_3_) | copy-start | bytes 3145732
  92.5 31.2 %copy-start.1 = (f32[4,128,1024]{2,1,0:T(8,128)}, f32[4,128,1024]{2,1,0:T(8,128)S(1)}, u32[]{:S(2)}) copy-start(f32[4,128,1024]{2,1,0:T(8,128)S(1)} %collective-permute-done.8.refs_1_) | copy-start | bytes 6291460
  93.5 30.2 %copy-start.2 = (f32[4,128,1024]{2,1,0:T(8,128)}, f32[4,128,1024]{2,1,0:T(8,128)S(1)}, u32[]{:S(2)}) copy-start(f32[4,128,1024]{2,1,0:T(8,128)S(1)} %collective-permute-done.9.refs_2_) | copy-start | bytes 6291460
  93.5 11.1 %collective-permute-start.12 = (f32[4,136,1024]{2,1,0:T(8,128)}, f32[4,136,1024]{2,1,0:T(8,128)S(1)}, u32[]{:S(2)}, u32[]{:S(2)}) collective-permute-start(f32[4,136,1024]{2,1,0:T(8,128)} %get-tuple-element.54.mine), channel_id=1, source_target_pairs={{0,1},{1,0},{2,3},{3,2},{4,5},{5,4},{6,7},{7,6},{8,9},{9,8},{10,11... | collective-permute-start | bytes 6684680 | tf_op jit(solution)/shard_map/ppermute | solution.py:586
  94.7 31.1 %collective-permute-start.13 = (f32[2,128,1024]{2,1,0:T(8,128)}, f32[2,128,1024]{2,1,0:T(8,128)}, u32[]{:S(2)}, u32[]{:S(2)}) collective-permute-start(f32[2,128,1024]{2,1,0:T(8,128)} %slice.22), channel_id=1, source_target_pairs={{1,5},{3,7},{5,1},{7,3},{9,13},{11,15},{13,9},{15,11},{17,21},{19,... | collective-permute-start | bytes 3145736 | tf_op jit(solution)/shard_map/ppermute | solution.py:576
  97.9 27.9 %collective-permute-start.14 = (f32[2,128,1024]{2,1,0:T(8,128)}, f32[2,128,1024]{2,1,0:T(8,128)}, u32[]{:S(2)}, u32[]{:S(2)}) collective-permute-start(f32[2,128,1024]{2,1,0:T(8,128)} %slice.23), channel_id=1, source_target_pairs={{1,3},{3,1},{5,7},{7,5},{9,11},{11,9},{13,15},{15,13},{17,19},{19,... | collective-permute-start | bytes 3145736 | tf_op jit(solution)/shard_map/ppermute | solution.py:576
  100.1 39.4 %collective-permute-start.15 = (f32[128,2048]{1,0:T(8,128)}, f32[128,2048]{1,0:T(8,128)}, u32[]{:S(2)}, u32[]{:S(2)}) collective-permute-start(f32[128,2048]{1,0:T(8,128)} %get-tuple-element.51), channel_id=1, source_target_pairs={{1,17},{9,25},{17,1},{25,9},{3,19},{11,27},{19,3},{27,11},{5,21},{... | collective-permute-start | bytes 3145736 | tf_op jit(solution)/shard_map/ppermute | solution.py:580
  144.0 6.8 %collective-permute-start.17 = (f32[768,1024]{1,0:T(8,128)}, f32[768,1024]{1,0:T(8,128)S(1)}, u32[]{:S(2)}, u32[]{:S(2)}) collective-permute-start(f32[768,1024]{1,0:T(8,128)} %pick.1), channel_id=1, source_target_pairs={{1,0},{3,2},{5,4},{7,6},{9,8},{11,10},{13,12},{15,14},{17,16},{19,... | collective-permute-start | bytes 9437192 | tf_op jit(solution)/shard_map/ppermute | solution.py:589
  145.5 4.6 %collective-permute-start.18 = (f32[512,512]{1,0:T(8,128)S(1)}, f32[512,512]{1,0:T(8,128)S(1)}, u32[]{:S(2)}, u32[]{:S(2)}) collective-permute-start(f32[512,512]{1,0:T(8,128)S(1)} %copy-done.10), channel_id=1, source_target_pairs={{0,1},{2,3},{4,5},{6,7},{8,9},{10,11},{12,13},{14,15},{16,17},{18,... | collective-permute-start | bytes 3145736 | tf_op jit(solution)/shard_map/ppermute | solution.py:583
  (14 other events, 98.9 us)
